TPU v7x, 512 devices: a whole 4x4x16 slice. The times are simulated.
512 devices in a mesh: ctx: 16 (over z_lo, y), head: 32 (over z_hi, x, core).
Axes of the slice: x: 4, y: 4, z: 16 (z_hi: 4, z_lo: 4; z = z_hi * 4 + z_lo), core: 2. Of those that a mesh axis runs over, the one named last changes fastest.
Arguments:
- inputs: bfloat16 [2048, 8192], P('head', 'ctx'), may hold values from -6 to 6
- queries: bfloat16 [2048, 8192], P('ctx', 'head'), may hold values from -140 to 140
- keys: bfloat16 [2048, 1024], P('ctx'), may hold values from -6 to 6
- values: bfloat16 [2048, 1024], P('ctx'), may hold values from -6 to 6
- outputs: bfloat16 [2048, 8192], P('ctx', 'head'), may hold values from -0.59765625 to 0.59765625
- out_grad: bfloat16 [2048, 8192], P('ctx', 'head'), may hold values from -6 to 6
- block_mask: int32 [32, 32], replicated, may hold values from 0 to 1, as said below
Outputs:
- q_grad: bfloat16 [2048, 8192], P('ctx', 'head')
- kv_grad: bfloat16 [2048, 2048], P('ctx', 'head')
- weight_q_grad: bfloat16 [8192, 8192], P('ctx', 'head')
- weight_kv_grad: bfloat16 [8192, 2048], P('ctx', 'head')
Inputs may be any that keep to these rules, and one draw needn't show every extreme that they name: block_mask is 1 on its diagonal and 0 above it; below it entries are 0 or 1.
All inputs are finite; a program needn't handle non-finite values.
Results may differ from a plain program's by a relative error of at most 0.022.
Values may be sent and summed in bfloat16 or wider, within the bound.
A program may use at most 64 MiB of HBM per device.

v0:
```python
import jax
import jax.numpy as jnp
from jax import lax
from jax.sharding import PartitionSpec as P

HD = 128
BLK = 64


def swapped(value, axis, distance):
    mask = 2**distance
    pairs = [(source, source ^ mask) for source in range(lax.axis_size(axis))]
    return lax.ppermute(value, axis, pairs)


def contract_last(left, right):
    return lax.dot_general(
        left, right, (((1,), (1,)), ((), ())), preferred_element_type=jnp.float32
    )


def contract_first(left, right):
    return lax.dot_general(
        left, right, (((0,), (0,)), ((), ())), preferred_element_type=jnp.float32
    )


def attend(query_slab, grad_slab, out_slab, query_pos, all_keys, all_values, block_mask, totals):
    shard_rows = all_keys.shape[0] // lax.axis_size("ctx")
    score_scale = HD ** (-0.5)
    row_count = query_pos.shape[0]
    block_pick = jax.nn.one_hot(query_pos // BLK, block_mask.shape[0], dtype=jnp.float32)
    mask_rows = jnp.dot(block_pick, block_mask.astype(jnp.float32))
    shard_count = query_pos[row_count - 1] // shard_rows + 1
    blocks_per = shard_rows // BLK

    def shard_allowed(shard):
        key_pos = shard * shard_rows + jnp.arange(shard_rows)
        columns = lax.dynamic_slice_in_dim(mask_rows, shard * blocks_per, blocks_per, 1)
        wide_mask = jnp.repeat(columns, BLK, axis=1)
        return (key_pos[None, :] <= query_pos[:, None]) & (wide_mask > 0.5)

    key_total, value_total = totals
    grads = []
    for head_slot in range(query_slab.shape[1] // HD):
        column = head_slot * HD
        query_head = query_slab[:, column : column + HD]
        grad_head = grad_slab[:, column : column + HD]
        out_head = out_slab[:, column : column + HD]

        def stats_step(shard, carry):
            run_max, run_sum = carry
            key_shard = lax.dynamic_slice_in_dim(all_keys, shard * shard_rows, shard_rows, 0)
            scores = jnp.where(
                shard_allowed(shard), contract_last(query_head, key_shard) * score_scale, -jnp.inf
            )
            new_max = jnp.maximum(run_max, jnp.max(scores, axis=1, keepdims=True))
            new_sum = run_sum * jnp.exp(run_max - new_max) + jnp.sum(
                jnp.exp(scores - new_max), axis=1, keepdims=True
            )
            return (new_max, new_sum)

        start_stats = (
            jnp.full((row_count, 1), -1e30, jnp.float32),
            jnp.zeros((row_count, 1), jnp.float32),
        )
        row_max, row_sum = lax.fori_loop(0, shard_count, stats_step, start_stats)
        log_total = row_max + jnp.log(row_sum)
        delta = jnp.sum(
            grad_head.astype(jnp.float32) * out_head.astype(jnp.float32), axis=1, keepdims=True
        )

        def grad_step(shard, carry):
            query_acc, key_acc, value_acc = carry
            key_shard = lax.dynamic_slice_in_dim(all_keys, shard * shard_rows, shard_rows, 0)
            value_shard = lax.dynamic_slice_in_dim(all_values, shard * shard_rows, shard_rows, 0)
            scores = jnp.where(
                shard_allowed(shard), contract_last(query_head, key_shard) * score_scale, -jnp.inf
            )
            probs = jnp.exp(scores - log_total)
            probs_low = probs.astype(jnp.bfloat16)
            dprobs = contract_last(grad_head, value_shard)
            dscores = (probs * (dprobs - delta) * score_scale).astype(jnp.bfloat16)
            query_acc = query_acc + jnp.dot(dscores, key_shard, preferred_element_type=jnp.float32)
            old_keys = lax.dynamic_slice_in_dim(key_acc, shard * shard_rows, shard_rows, 0)
            key_acc = lax.dynamic_update_slice_in_dim(
                key_acc, old_keys + contract_first(dscores, query_head), shard * shard_rows, 0
            )
            old_values = lax.dynamic_slice_in_dim(value_acc, shard * shard_rows, shard_rows, 0)
            value_acc = lax.dynamic_update_slice_in_dim(
                value_acc, old_values + contract_first(probs_low, grad_head), shard * shard_rows, 0
            )
            return (query_acc, key_acc, value_acc)

        start_grads = (jnp.zeros((row_count, HD), jnp.float32), key_total, value_total)
        query_acc, key_total, value_total = lax.fori_loop(0, shard_count, grad_step, start_grads)
        grads.append(query_acc.astype(jnp.bfloat16))
    return (jnp.concatenate(grads, axis=1), (key_total, value_total))


def per_device(inputs, queries, keys, values, outputs, out_grad, block_mask):
    tok_rows = queries.shape[0]
    head_count = lax.axis_size("head")
    per_group = head_count // (keys.shape[1] // HD)
    head_index = lax.axis_index("head")
    ctx_index = lax.axis_index("ctx")
    kv_group = head_index // per_group
    key_rows = lax.dynamic_slice_in_dim(keys, kv_group * HD, HD, 1)
    value_rows = lax.dynamic_slice_in_dim(values, kv_group * HD, HD, 1)
    all_keys, all_values = (
        lax.all_gather(key_rows, "ctx", axis=0, tiled=True),
        lax.all_gather(value_rows, "ctx", axis=0, tiled=True),
    )
    seq_total = all_keys.shape[0]
    totals = (jnp.zeros((seq_total, HD), jnp.float32), jnp.zeros((seq_total, HD), jnp.float32))
    own_pos = ctx_index * tok_rows + jnp.arange(tok_rows)
    q_grad, totals = attend(
        queries, out_grad, outputs, own_pos, all_keys, all_values, block_mask, totals
    )
    kv_term = jnp.concatenate([totals[0], totals[1]], axis=1)
    ctx_summed = lax.psum_scatter(kv_term, "ctx", scatter_dimension=0, tiled=True).astype(
        jnp.bfloat16
    )
    group_part = ctx_summed.astype(jnp.float32)
    bit_count = per_group.bit_length() - 1
    for bit_index in reversed(range(bit_count)):
        half_width = group_part.shape[1] // 2
        my_side = head_index >> bit_index & 1
        kept_half = lax.dynamic_slice_in_dim(group_part, my_side * half_width, half_width, 1)
        sent_half = lax.dynamic_slice_in_dim(group_part, (1 - my_side) * half_width, half_width, 1)
        group_part = kept_half + swapped(sent_half.astype(jnp.bfloat16), "head", bit_index).astype(
            sent_half.dtype
        )
    kv_grad = group_part.astype(jnp.bfloat16)
    query_all, kv_all = (
        lax.all_gather(q_grad, "ctx", axis=0, tiled=True),
        lax.all_gather(kv_grad, "ctx", axis=0, tiled=True),
    )
    piece = lax.all_gather(inputs, "head", axis=0, tiled=True)
    weight_q = contract_first(piece, query_all)
    weight_kv = contract_first(piece, kv_all)
    return (q_grad, kv_grad, weight_q.astype(jnp.bfloat16), weight_kv.astype(jnp.bfloat16))


def solution(mesh):
    in_specs = (
        P("head", "ctx"),
        P("ctx", "head"),
        P("ctx", None),
        P("ctx", None),
        P("ctx", "head"),
        P("ctx", "head"),
        P(),
    )
    out_specs = (P("ctx", "head"), P("ctx", "head"), P("ctx", "head"), P("ctx", "head"))
    return jax.shard_map(
        per_device, mesh=mesh, in_specs=in_specs, out_specs=out_specs, check_vma=False
    )
```

profile of v0, /device:TPU:6, one launch (start us, length us, event | category | flops | bytes accessed | tf_op | source)
XLA Modules:
  0.0 478.6 jit_solution(3118299841790346627)
XLA Ops:
  9.9 46.7 %all_gather.15 = bf16[2048,128]{1,0:T(8,128)(2,1)S(1)} all-gather(bf16[128,128]{1,0:T(8,128)(2,1)S(1)} %constant_dynamic-slice_fusion.3), channel_id=1, replica_groups=mesh['ctx'=16,'head'=32] {'ctx'}, dimensions={0}, use_global_device_ids=true | all-gather | bytes 557056 | tf_op jit(solution)/shard_map/all_gather | solution.py:111
  57.2 0.9 fusion.54
  58.1 0.8 fusion.59
  59.4 0.8 constant_dynamic-slice_fusion.2
  60.2 47.8 %all_gather.16 = bf16[2048,128]{1,0:T(8,128)(2,1)} all-gather(bf16[128,128]{1,0:T(8,128)(2,1)S(1)} %constant_dynamic-slice_fusion.2), channel_id=1, replica_groups=mesh['ctx'=16,'head'=32] {'ctx'}, dimensions={0}, use_global_device_ids=true | all-gather | bytes 557056 | tf_op jit(solution)/shard_map/all_gather | solution.py:112
  108.3 1.7 while.57
  108.6 0.9 fusion.127
  110.7 1.7 while.59
  111.0 0.9 fusion.144
  113.1 1.5 pad_maximum_fusion
  114.6 0.7 copy-done.2
  115.4 0.6 pad_maximum_fusion.1
  116.1 0.7 all-gather.5.cloned.1.call-update
  116.8 144.9 %reduce-scatter.2.cloned.1.call-done = f32[128,256]{0,1:T(8,128)} async-done(((f32[2048,256]{0,1:T(8,128)}), f32[128,256]{0,1:T(8,128)}) %reduce-scatter.2.cloned.1.call-update) | async-done | bytes 131088 | tf_op jit(solution)/shard_map/reduce_scatter | solution.py:121
  261.7 0.9 convert_convert_fusion
  262.6 2.8 collective-permute-start
  265.5 2.9 collective-permute-done
  268.4 1.9 collective-permute-start.1
  270.4 76.1 %all-gather.3.cloned.1.call-done = bf16[2048,256]{1,0:T(8,128)(2,1)} async-done(((bf16[128,256]{1,0:T(8,128)(2,1)}), bf16[2048,256]{1,0:T(8,128)(2,1)}) %all-gather.3.cloned.1.call-update) | async-done | bytes 1048592 | tf_op jit(solution)/shard_map/all_gather | solution.py:136
  346.5 80.0 %all-gather.5.cloned.1.call-done = bf16[2048,512]{1,0:T(8,128)(2,1)} async-done(((bf16[64,512]{1,0:T(8,128)(2,1)}), bf16[2048,512]{1,0:T(8,128)(2,1)}) %all-gather.5.cloned.1.call-update) | async-done | bytes 2097168 | tf_op jit(solution)/shard_map/all_gather | solution.py:139
  426.5 2.8 fusion.52
  429.2 0.8 copy.15
  430.1 40.9 %all_gather.19 = bf16[2048,64]{0,1:T(8,128)(2,1)S(1)} all-gather(bf16[128,64]{0,1:T(8,128)(2,1)S(1)} %add_convert_fusion), channel_id=1, replica_groups=mesh['ctx'=16,'head'=32] {'ctx'}, dimensions={0}, use_global_device_ids=true | all-gather | bytes 278528 | tf_op jit(solution)/shard_map/all_gather | solution.py:137
  471.0 1.1 fusion.53
  (73 shorter events, 4.9 us)
Async XLA Ops:
  7.2 2.7 copy-start
  7.2 100.8 %copy-start.4 = (bf16[128,256]{1,0:T(8,128)(2,1)S(1)}, bf16[128,256]{1,0:T(8,128)(2,1)}, u32[]{:S(2)}) copy-start(bf16[128,256]{1,0:T(8,128)(2,1)} %param.20) | copy-start | bytes 196612
  7.2 100.8 %copy-start.5 = (bf16[128,256]{1,0:T(8,128)(2,1)S(1)}, bf16[128,256]{1,0:T(8,128)(2,1)}, u32[]{:S(2)}) copy-start(bf16[128,256]{1,0:T(8,128)(2,1)} %param.19) | copy-start | bytes 196612
  7.2 254.5 %reduce-scatter.2.cloned.1.call-start = ((), (), s32[]{:S(2)}) async-start(), calls=%async_computation.1 | async-start | bytes 2228224 | tf_op jit(solution)/shard_map/reduce_scatter | solution.py:121
  110.0 0.6 copy-start.1
  114.5 0.8 copy-start.2
  114.5 231.9 %all-gather.3.cloned.1.call-start = ((), (), s32[]{:S(2)}) async-start(), calls=%async_computation.2 | async-start | bytes 1114112 | tf_op jit(solution)/shard_map/all_gather | solution.py:136
  116.0 310.4 %all-gather.5.cloned.1.call-start = ((), (), s32[]{:S(2)}) async-start(), calls=%async_computation.3 | async-start | bytes 2162688 | tf_op jit(solution)/shard_map/all_gather | solution.py:139
  262.6 5.8 %collective-permute-start = (bf16[128,128]{0,1:T(8,128)(2,1)S(1)}, bf16[128,128]{0,1:T(8,128)(2,1)S(1)}, u32[]{:S(2)}, u32[]{:S(2)}) collective-permute-start(bf16[128,128]{0,1:T(8,128)(2,1)S(1)} %dynamic-slice_convert_fusion), channel_id=1, source_target_pairs={{0,2},{1,3},{2,0},{3,1},{4,6},{5,7},{6,4},{7,5},{8,10},{9,11},{10,... | collective-permute-start | bytes 98312 | tf_op jit(solution)/shard_map/ppermute | solution.py:13
  268.4 161.6 %collective-permute-start.1 = (bf16[128,64]{0,1:T(8,128)(2,1)S(1)}, bf16[128,64]{0,1:T(8,128)(2,1)S(1)}, u32[]{:S(2)}, u32[]{:S(2)}) collective-permute-start(bf16[128,64]{0,1:T(8,128)(2,1)S(1)} %dynamic-slice_convert_fusion.1), channel_id=1, source_target_pairs={{0,1},{1,0},{2,3},{3,2},{4,5},{5,4},{6,7},{7,6},{8,9},{9,8},{10,11... | collective-permute-start | bytes 49160 | tf_op jit(solution)/shard_map/ppermute | solution.py:13
  426.5 44.5 %copy-start.3 = (bf16[2048,512]{1,0:T(8,128)(2,1)S(1)}, bf16[2048,512]{1,0:T(8,128)(2,1)}, u32[]{:S(2)}) copy-start(bf16[2048,512]{1,0:T(8,128)(2,1)} %all-gather.5.cloned.1.call-done) | copy-start | bytes 6291460
  430.1 42.0 %copy-start.6 = (bf16[128,64]{0,1:T(8,128)(2,1)}, bf16[128,64]{0,1:T(8,128)(2,1)S(1)}, u32[]{:S(2)}) copy-start(bf16[128,64]{0,1:T(8,128)(2,1)S(1)} %add_convert_fusion) | copy-start | bytes 49156
Sparse Core Ops, SparseCore 0:
  114.7 146.9 reduce-scatter.1
  264.3 82.1 all-gather.2
  349.6 76.7 all-gather.4
where the time goes:
time: 481 us; the launch traced here: 479 us
  waiting for transfers between devices  305 us (63%)
  blocking collectives  135 us (28%)
  between operations  16.7 us (3%)
  matrix products  8.26 us (2%)
  starting transfers between devices  4.89 us (1%)
  local copies, waits for them, and re-layouts  4.83 us (1%)
    reduce_scatter x1, waiting for transfers between devices, per_device(): lax.psum_scatter(kv_term, 'ctx', scatter_dimension=0, tiled=True)  145 us
    all_gather x1, waiting for transfers between devices, per_device(): piece = lax.all_gather(inputs, 'head', axis=0, tiled=True)  80 us
    all_gather x1, waiting for transfers between devices, per_device(): lax.all_gather(q_grad, 'ctx', axis=0, tiled=True)  76.1 us
    all_gather x1, blocking collectives, per_device(): lax.all_gather(value_rows, 'ctx', axis=0, tiled=True)  47.8 us
    all_gather x1, blocking collectives, per_device(): lax.all_gather(key_rows, 'ctx', axis=0, tiled=True)  46.7 us
    all_gather x1, blocking collectives, per_device(): lax.all_gather(kv_grad, 'ctx', axis=0, tiled=True)  40.9 us
  transfers between devices with their start and end apart: 5, of which 4 were waited for; matrix products, arithmetic and copies ran while one was open for 1% of the time, Pallas kernels for 0%

commit v1 on v0

v1 whole, which is shorter than its diff:
```python
import functools

import jax
import jax.numpy as jnp
from jax import lax
from jax.experimental import pallas as pl
from jax.experimental.pallas import tpu as pltpu
from jax.sharding import PartitionSpec as P

HD = 128
BLK = 64
TOK = 2048
SHARD = 128
CHUNK = 256
MESH = pl.DeviceIdType.MESH
NEG = -1e30
F32 = jnp.float32
BF16 = jnp.bfloat16

PEERS = (
    [(d, 0, 0, 0, 0) for d in (1, 2, 3)]
    + [(0, d, 0, 0, 0) for d in (1, 2, 3)]
    + [(0, 0, d, 0, 0) for d in (1, 2, 3)]
    + [(0, 0, 0, d, 0) for d in (1, 2, 3)]
    + [(0, 0, 0, 0, 1)]
)


def dot(left, right):
    return lax.dot_general(left, right, (((1,), (0,)), ((), ())), preferred_element_type=F32)


def dot_t(left, right):
    return lax.dot_general(left, right, (((1,), (1,)), ((), ())), preferred_element_type=F32)


def stacked(value):
    return jnp.concatenate([value[:, :HD], value[:, HD:]], axis=0)


def body(
    inputs, queries, keys, values, outputs, out_grad, block_mask,
    q_out, kv_out, wq_out, wkv_out,
    act, kv_all, q_all, g_all, scores, probs, dsc, bias,
    sib_send, sib_recv, own, y_send, y_recv, zx_send, zx_recv,
    send_sem, recv_sem, local_sem,
):
    ctx = lax.axis_index("ctx")
    head = lax.axis_index("head")
    z, y = ctx // 4, ctx % 4
    zh, x, core = head // 8, (head // 2) % 4, head % 2
    sib = 1 - core
    side = x % 2
    group = head // 4

    def at(dz=0, dy=0, dzh=0, dx=0, dk=0):
        return (
            ((z + dz) % 4) * 4 + (y + dy) % 4,
            ((zh + dzh) % 4) * 8 + ((x + dx) % 4) * 2 + (core + dk) % 2,
        )

    def flip(dz):
        return (((z + dz) % 4) * 4 + y, zh * 8 + (x + 1 - 2 * side) * 2 + core)

    counter = [0]
    sends = []

    def slots(count):
        first = counter[0]
        counter[0] += count
        return first

    def copy(src, dst, slot, device):
        return pltpu.make_async_remote_copy(
            src_ref=src, dst_ref=dst, send_sem=send_sem.at[slot], recv_sem=recv_sem.at[slot],
            device_id=device, device_id_type=MESH,
        )

    def send(src, dst, slot, device):
        item = copy(src, dst, slot, device)
        item.start()
        sends.append(item)

    def arrive(dst, slot):
        copy(dst, dst, slot, at(dk=1)).wait_recv()

    own_rows = pl.ds(pl.multiple_of(ctx * SHARD, SHARD), SHARD)
    own_cols = pl.ds(pl.multiple_of(group * HD, HD), HD)
    own_act = pl.ds(pl.multiple_of(head * 64, 64), 64)
    loads = [
        pltpu.make_async_copy(keys.at[:, own_cols], kv_all.at[0, own_rows], local_sem.at[0]),
        pltpu.make_async_copy(values.at[:, own_cols], kv_all.at[1, own_rows], local_sem.at[1]),
        pltpu.make_async_copy(inputs, act.at[own_act], local_sem.at[2]),
    ]
    for item in loads:
        item.start()

    barrier = pltpu.get_barrier_semaphore()
    for offset in PEERS:
        pl.semaphore_signal(barrier, inc=1, device_id=at(*offset), device_id_type=MESH)
    for dz in (1, 2, 3):
        pl.semaphore_signal(barrier, inc=1, device_id=flip(dz), device_id_type=MESH)
    for item in loads:
        item.wait()
    pl.semaphore_wait(barrier, len(PEERS) + 3)

    class Gather:
        def __init__(self, place):
            self.place = place
            self.first = slots(16)

        def shard(self, dz, dy):
            return self.place(((z - dz) % 4) * 4 + (y - dy) % 4)

        def start(self):
            for dz in (1, 3, 2):
                send(self.shard(0, 0), self.shard(0, 0), self.first + dz * 4, at(dz=dz))
            self.along_y(0)

        def along_y(self, dz):
            for dy in (1, 3, 2):
                send(self.shard(dz, 0), self.shard(dz, 0), self.first + dz * 4 + dy, at(dy=dy))

        def wait(self, dz, dy):
            arrive(self.shard(dz, dy), self.first + dz * 4 + dy)

    def rows_of(index):
        return pl.ds(pl.multiple_of(index * SHARD, SHARD), SHARD)

    kv_gather = Gather(lambda index: kv_all.at[core, rows_of(index)])
    kv_gather.start()
    sib_first = slots(16)

    def to_sibling(dz, dy):
        part = kv_gather.shard(dz, dy)
        send(part, part, sib_first + dz * 4 + dy, at(dk=1))

    row_ids = lax.broadcasted_iota(jnp.int32, (2 * SHARD, CHUNK), 0) % SHARD + ctx * SHARD
    pick = (
        lax.broadcasted_iota(jnp.int32, (2 * SHARD, 32), 1)
        == (lax.broadcasted_iota(jnp.int32, (2 * SHARD, 32), 0) % SHARD + ctx * SHARD) // BLK
    )
    mask_rows = dot(pick.astype(BF16), block_mask[...].astype(BF16)).astype(BF16)

    def bias_step(step, carry):
        cols = pl.ds(pl.multiple_of(step * CHUNK, CHUNK), CHUNK)
        col_ids = lax.broadcasted_iota(jnp.int32, (2 * SHARD, CHUNK), 1) + step * CHUNK
        spread = (
            (lax.broadcasted_iota(jnp.int32, (32, CHUNK), 1) + step * CHUNK) // BLK
            == lax.broadcasted_iota(jnp.int32, (32, CHUNK), 0)
        )
        wide = dot(mask_rows, spread.astype(BF16))
        bias[:, cols] = jnp.where((wide > 0.5) & (col_ids <= row_ids), 0.0, NEG)
        return carry

    lax.fori_loop(0, TOK // CHUNK, bias_step, 0)
    query = stacked(queries[...])
    grad = stacked(out_grad[...])
    delta = jnp.sum(grad.astype(F32) * stacked(outputs[...]).astype(F32), axis=1, keepdims=True)

    for dz in (1, 3, 2):
        kv_gather.wait(dz, 0)
        kv_gather.along_y(dz)
        to_sibling(dz, 0)

    act_first = slots(16)
    act_sib = slots(16)

    def act_shard(dzh, dx):
        index = ((zh - dzh) % 4) * 8 + ((x - dx) % 4) * 2 + core
        return act.at[pl.ds(pl.multiple_of(index * 64, 64), 64)]

    def act_from_sibling(dzh, dx):
        index = ((zh - dzh) % 4) * 8 + ((x - dx) % 4) * 2 + sib
        return act.at[pl.ds(pl.multiple_of(index * 64, 64), 64)]

    def act_along_x(dzh):
        for dx in (1, 3, 2):
            send(act_shard(dzh, 0), act_shard(dzh, 0), act_first + dzh * 4 + dx, at(dx=dx))
        act_to_sibling(dzh, 0)

    def act_to_sibling(dzh, dx):
        send(act_shard(dzh, dx), act_shard(dzh, dx), act_sib + dzh * 4 + dx, at(dk=1))

    for dzh in (1, 3, 2):
        send(act_shard(0, 0), act_shard(0, 0), act_first + dzh * 4, at(dzh=dzh))
    act_along_x(0)

    for dz in range(4):
        for dy in (1, 3, 2):
            kv_gather.wait(dz, dy)
            to_sibling(dz, dy)
    for dz in range(4):
        for dy in range(4):
            if dz or dy:
                index = ((z - dz) % 4) * 4 + (y - dy) % 4
                arrive(kv_all.at[sib, rows_of(index)], sib_first + dz * 4 + dy)

    scale = HD ** -0.5

    def score_step(step, top):
        cols = pl.ds(pl.multiple_of(step * CHUNK, CHUNK), CHUNK)
        part = dot_t(query, kv_all[0, cols, :]) * scale + bias[:, cols]
        scores[:, cols] = part
        return jnp.maximum(top, jnp.maximum(part[:, :HD], part[:, HD:]))

    top = lax.fori_loop(0, TOK // CHUNK, score_step, jnp.full((2 * SHARD, HD), NEG, F32))
    row_max = jnp.max(top, axis=1, keepdims=True)

    def prob_step(step, total):
        cols = pl.ds(pl.multiple_of(step * CHUNK, CHUNK), CHUNK)
        part = jnp.exp(scores[:, cols] - row_max)
        slope = dot_t(grad, kv_all[1, cols, :])
        probs[:, cols] = part.astype(BF16)
        dsc[:, cols] = (part * (slope - delta)).astype(BF16)
        return total + part[:, :HD] + part[:, HD:]

    total = lax.fori_loop(0, TOK // CHUNK, prob_step, jnp.zeros((2 * SHARD, HD), F32))
    inverse = 1.0 / jnp.sum(total, axis=1, keepdims=True)

    def mine_first(value):
        turned = value.T
        low, high = turned[:64], turned[64:]
        return jnp.concatenate(
            [jnp.where(core == 0, low, high), jnp.where(core == 0, high, low)], axis=0
        ).astype(BF16)

    query_t = mine_first(query.astype(F32) * (inverse * scale))
    grad_t = mine_first(grad.astype(F32) * inverse)

    def term_step(step, carry):
        cols = pl.ds(pl.multiple_of(step * CHUNK, CHUNK), CHUNK)
        key_part = dot(query_t, dsc[:, cols])
        value_part = dot(grad_t, probs[:, cols])
        for half in range(2):
            index = step * 2 + half
            block = (index % 4) * 4 + index // 4
            lanes = slice(half * HD, (half + 1) * HD)
            own[block, 0] = key_part[:64, lanes]
            own[block, 1] = value_part[:64, lanes]
            sib_send[block, 0] = key_part[64:, lanes].astype(BF16)
            sib_send[block, 1] = value_part[64:, lanes].astype(BF16)
        return carry

    lax.fori_loop(0, TOK // CHUNK, term_step, 0)
    core_slot = slots(1)
    send(sib_send, sib_recv, core_slot, at(dk=1))

    query_grad = dot(dsc[...], kv_all[0]) * (inverse * scale)
    q_out[:, :HD] = query_grad[:SHARD].astype(BF16)
    q_out[:, HD:] = query_grad[SHARD:].astype(BF16)
    own_lanes = pl.ds(pl.multiple_of(ctx * SHARD, SHARD), SHARD)
    q_all[:HD, own_lanes] = query_grad[:SHARD].T.astype(BF16)
    q_all[HD:, own_lanes] = query_grad[SHARD:].T.astype(BF16)

    arrive(sib_recv, core_slot)
    y_slot = slots(4)
    for dy in (1, 3, 2):
        dest = (y + dy) % 4

        def add_step(step, carry):
            block = dest * 4 + step
            y_send[dy - 1, step] = (own[block] + sib_recv[block].astype(F32)).astype(BF16)
            return carry

        lax.fori_loop(0, 4, add_step, 0)
        send(y_send.at[dy - 1], y_recv.at[dy - 1], y_slot + dy, at(dy=dy))

    def lanes_of(index):
        return pl.ds(pl.multiple_of(index * SHARD, SHARD), SHARD)

    q_gather = Gather(lambda index: q_all.at[:, lanes_of(index)])
    q_gather.start()

    for dzh in (1, 3, 2):
        arrive(act_shard(dzh, 0), act_first + dzh * 4)
        act_along_x(dzh)

    for dy in (1, 3, 2):
        arrive(y_recv.at[dy - 1], y_slot + dy)

    def y_sum(step, carry):
        block = y * 4 + step
        value = own[block] + sib_recv[block].astype(F32)
        for dy in (1, 2, 3):
            value = value + y_recv[dy - 1, step].astype(F32)
        own[block] = value
        zx_send[step] = value.astype(BF16)
        return carry

    lax.fori_loop(0, 4, y_sum, 0)

    zx_slot = slots(8)
    for dz in (1, 3, 2, 0):
        for dx in (0, 1):
            if dz or dx:
                part = side if dx == 0 else 1 - side
                slot = dz * 2 + dx
                send(
                    zx_send.at[(z + dz) % 4, part], zx_recv.at[slot], zx_slot + slot,
                    flip(dz) if dx else at(dz=dz),
                )

    for dz in (1, 3, 2):
        q_gather.wait(dz, 0)
        q_gather.along_y(dz)

    kv_sum = own[y * 4 + z, side]
    for slot in range(1, 8):
        arrive(zx_recv.at[slot], zx_slot + slot)
    for slot in range(1, 8):
        kv_sum = kv_sum + zx_recv[slot].astype(F32)
    g_all[:, own_lanes] = kv_sum.astype(BF16)
    g_gather = Gather(lambda index: g_all.at[:, lanes_of(index)])
    g_gather.start()
    kv_out[...] = kv_sum.T.astype(BF16)

    for dzh in range(4):
        for dx in (1, 3, 2):
            arrive(act_shard(dzh, dx), act_first + dzh * 4 + dx)
            act_to_sibling(dzh, dx)

    for dz in (1, 3, 2):
        g_gather.wait(dz, 0)
        g_gather.along_y(dz)

    for dz in range(4):
        for dy in (1, 3, 2):
            q_gather.wait(dz, dy)
    for dzh in range(4):
        for dx in range(4):
            arrive(act_from_sibling(dzh, dx), act_sib + dzh * 4 + dx)
    wq_out[...] = dot(q_all[...], act[...]).T.astype(BF16)

    for dz in range(4):
        for dy in (1, 3, 2):
            g_gather.wait(dz, dy)
    wkv_out[...] = dot(g_all[...], act[...]).T.astype(BF16)

    for item in sends:
        item.wait_send()


def per_device(inputs, queries, keys, values, outputs, out_grad, block_mask):
    vmem = pl.BlockSpec(memory_space=pltpu.VMEM)
    anywhere = pl.BlockSpec(memory_space=pl.ANY)
    return pl.pallas_call(
        body,
        name="attention_backward",
        out_shape=(
            jax.ShapeDtypeStruct((SHARD, 256), BF16),
            jax.ShapeDtypeStruct((SHARD, 64), BF16),
            jax.ShapeDtypeStruct((512, 256), BF16),
            jax.ShapeDtypeStruct((512, 64), BF16),
        ),
        in_specs=[anywhere, vmem, anywhere, anywhere, vmem, vmem, vmem],
        out_specs=(vmem, vmem, vmem, vmem),
        scratch_shapes=[
            pltpu.VMEM((TOK, 512), BF16),
            pltpu.VMEM((2, TOK, HD), BF16),
            pltpu.VMEM((256, TOK), BF16),
            pltpu.VMEM((64, TOK), BF16),
            pltpu.VMEM((256, TOK), F32),
            pltpu.VMEM((256, TOK), BF16),
            pltpu.VMEM((256, TOK), BF16),
            pltpu.VMEM((256, TOK), F32),
            pltpu.VMEM((16, 2, 64, HD), BF16),
            pltpu.VMEM((16, 2, 64, HD), BF16),
            pltpu.VMEM((16, 2, 64, HD), F32),
            pltpu.VMEM((3, 4, 2, 64, HD), BF16),
            pltpu.VMEM((3, 4, 2, 64, HD), BF16),
            pltpu.VMEM((4, 2, 64, HD), BF16),
            pltpu.VMEM((8, 64, HD), BF16),
            pltpu.SemaphoreType.DMA((112,)),
            pltpu.SemaphoreType.DMA((112,)),
            pltpu.SemaphoreType.DMA((3,)),
        ],
        compiler_params=pltpu.CompilerParams(
            collective_id=0, has_side_effects=True, vmem_limit_bytes=48 << 20
        ),
        cost_estimate=pl.CostEstimate(
            flops=1_400_000_000, bytes_accessed=4 << 20, transcendentals=256 * TOK
        ),
    )(inputs, queries, keys, values, outputs, out_grad, block_mask)


def solution(mesh):
    in_specs = (
        P("head", "ctx"),
        P("ctx", "head"),
        P("ctx", None),
        P("ctx", None),
        P("ctx", "head"),
        P("ctx", "head"),
        P(),
    )
    out_specs = (P("ctx", "head"), P("ctx", "head"), P("ctx", "head"), P("ctx", "head"))
    return jax.shard_map(
        per_device, mesh=mesh, in_specs=in_specs, out_specs=out_specs, check_vma=False
    )
```

time: 481 us -> 70.2 us (0.15)
  waiting for transfers between devices: 305 us -> 0 us
  blocking collectives: 135 us -> 0 us
  Pallas kernels: 0 us -> 60.4 us
  between operations: 16.7 us -> 0.66 us
  matrix products: 8.26 us -> 0 us
  starting transfers between devices: 4.89 us -> 0 us
    all_gather x2 -> x0, waiting for transfers between devices: 156 us -> none  [the longest x1 80 us: per_device(): piece = lax.all_gather(inputs, 'head', axis=0, tiled=True)]
    reduce_scatter x1 -> x0, waiting for transfers between devices: 145 us -> none  [per_device(): lax.psum_scatter(kv_term, 'ctx', scatter_dimension=0, tiled=True)]
    all_gather x3 -> x0, blocking collectives: 135 us -> none  [the longest x1 47.8 us: per_device(): lax.all_gather(value_rows, 'ctx', axis=0, tiled=True)]
    pallas_call x0 -> x1, Pallas kernels: none -> 60.4 us  [per_device(): pl.pallas_call(body, name='attention_backward', out_shape=(jax.ShapeDtype...]
    dot_general x15 -> x0, matrix products: 8.26 us -> none  [the longest x6 4.43 us: contract_first(): lax.dot_general(left, right, (((0,), (0,)), ((), ())), preferred_element_...]
    unnamed x15 -> x16, local copies, waits for them, and re-layouts: 1.78 us -> 7.3 us
  transfers between devices with their start and end apart: 5 -> 0, of which waited for: 4 -> 0; matrix products, arithmetic and copies ran while one was open for 1% -> 0% of each run, Pallas kernels for 0% -> 0%
where the time goes in v1:
time: 70.2 us; the launch traced here: 69.8 us
  Pallas kernels  60.4 us (86%)
  local copies, waits for them, and re-layouts  8.72 us (12%)
    pallas_call x1, Pallas kernels, per_device(): pl.pallas_call(body, name='attention_backward', out_shape=(jax.ShapeDtype...  60.4 us
    unnamed x16, local copies, waits for them, and re-layouts  7.3 us
    pallas_call x2, local copies, waits for them, and re-layouts, per_device(): pl.pallas_call(body, name='attention_backward', out_shape=(jax.ShapeDtype...  1.42 us

profile of v1, /device:TPU:6, one launch (start us, length us, event | category | flops | bytes accessed | tf_op | source)
XLA Modules:
  0.0 69.8 jit_solution(15059845488819026310)
XLA Ops:
  0.6 0.0 copy-start
  0.6 0.9 %copy-done = bf16[128,1024]{1,0:T(8,128)(2,1)S(1)} copy-done((bf16[128,1024]{1,0:T(8,128)(2,1)S(1)}, bf16[128,1024]{1,0:T(8,128)(2,1)}, u32[]{:S(2)}) %copy-start) | copy-done | bytes 262168
  1.6 0.0 copy-start.1
  1.6 0.9 %copy-done.1 = bf16[128,1024]{1,0:T(8,128)(2,1)S(1)} copy-done((bf16[128,1024]{1,0:T(8,128)(2,1)S(1)}, bf16[128,1024]{1,0:T(8,128)(2,1)}, u32[]{:S(2)}) %copy-start.1) | copy-done | bytes 262168
  2.5 0.0 copy-start.2
  2.5 0.8 %copy-done.2 = bf16[64,512]{1,0:T(8,128)(2,1)S(1)} copy-done((bf16[64,512]{1,0:T(8,128)(2,1)S(1)}, bf16[64,512]{1,0:T(8,128)(2,1)}, u32[]{:S(2)}) %copy-start.2) | copy-done | bytes 65560
  3.4 0.0 copy-start.3
  3.4 0.8 %copy-done.3 = bf16[128,256]{1,0:T(8,128)(2,1)S(1)} copy-done((bf16[128,256]{1,0:T(8,128)(2,1)S(1)}, bf16[128,256]{1,0:T(8,128)(2,1)}, u32[]{:S(2)}) %copy-start.3) | copy-done | bytes 65560
  4.2 0.0 copy-start.4
  4.2 0.8 %copy-done.4 = bf16[128,256]{1,0:T(8,128)(2,1)S(1)} copy-done((bf16[128,256]{1,0:T(8,128)(2,1)S(1)}, bf16[128,256]{1,0:T(8,128)(2,1)}, u32[]{:S(2)}) %copy-start.4) | copy-done | bytes 65560
  5.1 0.0 copy-start.5
  5.1 0.8 %copy-done.5 = bf16[128,256]{1,0:T(8,128)(2,1)S(1)} copy-done((bf16[128,256]{1,0:T(8,128)(2,1)S(1)}, bf16[128,256]{1,0:T(8,128)(2,1)}, u32[]{:S(2)}) %copy-start.5) | copy-done | bytes 65560
  5.9 0.0 copy-start.6
  5.9 0.7 %copy-done.6 = s32[32,32]{1,0:T(8,128)S(1)} copy-done((s32[32,32]{1,0:T(8,128)S(1)}, s32[32,32]{1,0:T(8,128)}, u32[]{:S(2)}) %copy-start.6) | copy-done | bytes 4120
  6.6 60.4 %attention_backward.1 = (bf16[128,256]{1,0:T(8,128)(2,1)S(1)}, bf16[128,64]{1,0:T(8,128)(2,1)S(1)}, bf16[512,256]{1,0:T(8,128)(2,1)S(1)}, bf16[512,64]{1,0:T(8,128)(2,1)S(1)}) custom-call(bf16[64,512]{1,0:T(8,128)(2,1)S(1)} %copy-done.2, bf16[128,256]{1,0:T(8,128)(2,1)S(1)} %copy-done.3, bf16[128,1024]{1,0:T(8,128)(2,1)S(1)} %copy-done, ...), custom_call_target="tpu_custom_call" | custom-call | flops 1400000000 | bytes 4194304 | tf_op jit(solution)/shard_map/attention_backward/pallas_call | solution.py:347
  67.1 0.7 copy.11
  67.8 0.7 %copy.12 = bf16[512,64]{0,1:T(8,128)(2,1)} copy(bf16[512,64]{1,0:T(8,128)(2,1)S(1)} %get-tuple-element.7) | data formatting | bytes 131072 | tf_op jit(solution)/shard_map/attention_backward/pallas_call | solution.py:347
  68.5 0.6 copy.15
  69.1 0.7 %copy.16 = bf16[512,256]{1,0:T(8,128)(2,1)} copy(bf16[512,256]{1,0:T(8,128)(2,1)S(1)} %get-tuple-element.14) | data formatting | bytes 524288
Async XLA Ops:
  0.6 1.0 %copy-start = (bf16[128,1024]{1,0:T(8,128)(2,1)S(1)}, bf16[128,1024]{1,0:T(8,128)(2,1)}, u32[]{:S(2)}) copy-start(bf16[128,1024]{1,0:T(8,128)(2,1)} %keys.1) | copy-start | bytes 786436
  1.6 0.9 %copy-start.1 = (bf16[128,1024]{1,0:T(8,128)(2,1)S(1)}, bf16[128,1024]{1,0:T(8,128)(2,1)}, u32[]{:S(2)}) copy-start(bf16[128,1024]{1,0:T(8,128)(2,1)} %values.1) | copy-start | bytes 786436
  2.5 0.8 %copy-start.2 = (bf16[64,512]{1,0:T(8,128)(2,1)S(1)}, bf16[64,512]{1,0:T(8,128)(2,1)}, u32[]{:S(2)}) copy-start(bf16[64,512]{1,0:T(8,128)(2,1)} %inputs.1) | copy-start | bytes 196612
  3.4 0.8 %copy-start.3 = (bf16[128,256]{1,0:T(8,128)(2,1)S(1)}, bf16[128,256]{1,0:T(8,128)(2,1)}, u32[]{:S(2)}) copy-start(bf16[128,256]{1,0:T(8,128)(2,1)} %queries.1) | copy-start | bytes 196612
  4.2 0.8 %copy-start.4 = (bf16[128,256]{1,0:T(8,128)(2,1)S(1)}, bf16[128,256]{1,0:T(8,128)(2,1)}, u32[]{:S(2)}) copy-start(bf16[128,256]{1,0:T(8,128)(2,1)} %outputs.1) | copy-start | bytes 196612
  5.1 0.8 %copy-start.5 = (bf16[128,256]{1,0:T(8,128)(2,1)S(1)}, bf16[128,256]{1,0:T(8,128)(2,1)}, u32[]{:S(2)}) copy-start(bf16[128,256]{1,0:T(8,128)(2,1)} %out_grad.1) | copy-start | bytes 196612
  5.9 0.7 %copy-start.6 = (s32[32,32]{1,0:T(8,128)S(1)}, s32[32,32]{1,0:T(8,128)}, u32[]{:S(2)}) copy-start(s32[32,32]{1,0:T(8,128)} %block_mask.1) | copy-start | bytes 12292

commit v2 on v1

--- a/solution.py
+++ b/solution.py
@@ -14,13 +14,13 @@
 CHUNK = 256
 MESH = pl.DeviceIdType.MESH
 NEG = -1e30
+VMEM_LIMIT = 60 << 20
 F32 = jnp.float32
 BF16 = jnp.bfloat16
 
 PEERS = (
     [(d, 0, 0, 0, 0) for d in (1, 2, 3)]
     + [(0, d, 0, 0, 0) for d in (1, 2, 3)]
-    + [(0, 0, d, 0, 0) for d in (1, 2, 3)]
     + [(0, 0, 0, d, 0) for d in (1, 2, 3)]
     + [(0, 0, 0, 0, 1)]
 )
@@ -41,9 +41,10 @@
 def body(
     inputs, queries, keys, values, outputs, out_grad, block_mask,
     q_out, kv_out, wq_out, wkv_out,
+    query_in, grad_in, out_in, mask_in,
     act, kv_all, q_all, g_all, scores, probs, dsc, bias,
     sib_send, sib_recv, own, y_send, y_recv, zx_send, zx_recv,
-    send_sem, recv_sem, local_sem,
+    send_sem, recv_sem, local_sem, ready_sem,
 ):
     ctx = lax.axis_index("ctx")
     head = lax.axis_index("head")
@@ -91,6 +92,10 @@
         pltpu.make_async_copy(keys.at[:, own_cols], kv_all.at[0, own_rows], local_sem.at[0]),
         pltpu.make_async_copy(values.at[:, own_cols], kv_all.at[1, own_rows], local_sem.at[1]),
         pltpu.make_async_copy(inputs, act.at[own_act], local_sem.at[2]),
+        pltpu.make_async_copy(block_mask, mask_in, local_sem.at[3]),
+        pltpu.make_async_copy(queries, query_in, local_sem.at[4]),
+        pltpu.make_async_copy(out_grad, grad_in, local_sem.at[5]),
+        pltpu.make_async_copy(outputs, out_in, local_sem.at[6]),
     ]
     for item in loads:
         item.start()
@@ -100,9 +105,19 @@
         pl.semaphore_signal(barrier, inc=1, device_id=at(*offset), device_id_type=MESH)
     for dz in (1, 2, 3):
         pl.semaphore_signal(barrier, inc=1, device_id=flip(dz), device_id_type=MESH)
-    for item in loads:
+    def rank_of(index):
+        return jnp.where(index < 2, index, 5 - index)
+
+    rank = rank_of(zh)
+    ranks = {dzh: rank_of((zh + dzh) % 4) for dzh in (1, 2, 3)}
+    for dzh in (1, 2, 3):
+        @pl.when(rank < ranks[dzh])
+        def _(dzh=dzh):
+            pl.semaphore_signal(barrier, inc=1, device_id=at(dzh=dzh), device_id_type=MESH)
+
+    for item in loads[:3]:
         item.wait()
-    pl.semaphore_wait(barrier, len(PEERS) + 3)
+    pl.semaphore_wait(barrier, len(PEERS) + 3 + rank)
 
     class Gather:
         def __init__(self, place):
@@ -135,12 +150,44 @@
         part = kv_gather.shard(dz, dy)
         send(part, part, sib_first + dz * 4 + dy, at(dk=1))
 
+    act_first = slots(16)
+    act_sib = slots(16)
+
+    def act_shard(dzh, dx):
+        index = ((zh - dzh) % 4) * 8 + ((x - dx) % 4) * 2 + core
+        return act.at[pl.ds(pl.multiple_of(index * 64, 64), 64)]
+
+    def act_from_sibling(dzh, dx):
+        index = ((zh - dzh) % 4) * 8 + ((x - dx) % 4) * 2 + sib
+        return act.at[pl.ds(pl.multiple_of(index * 64, 64), 64)]
+
+    def act_along_x(dzh):
+        for dx in (1, 3, 2):
+            send(act_shard(dzh, 0), act_shard(dzh, 0), act_first + dzh * 4 + dx, at(dx=dx))
+        act_to_sibling(dzh, 0)
+
+    def act_to_sibling(dzh, dx):
+        send(act_shard(dzh, dx), act_shard(dzh, dx), act_sib + dzh * 4 + dx, at(dk=1))
+
+    def act_along_z(dzh):
+        return copy(act_shard(0, 0), act_shard(0, 0), act_first + dzh * 4, at(dzh=dzh))
+
+    for dzh in (1, 3, 2):
+        sends.append(act_along_z(dzh))
+
+        @pl.when(rank > ranks[dzh])
+        def _(dzh=dzh):
+            pl.semaphore_signal(ready_sem.at[dzh], inc=1, device_id=at(dzh=dzh), device_id_type=MESH)
+            act_along_z(dzh).start()
+
+    for item in loads[3:]:
+        item.wait()
     row_ids = lax.broadcasted_iota(jnp.int32, (2 * SHARD, CHUNK), 0) % SHARD + ctx * SHARD
     pick = (
         lax.broadcasted_iota(jnp.int32, (2 * SHARD, 32), 1)
         == (lax.broadcasted_iota(jnp.int32, (2 * SHARD, 32), 0) % SHARD + ctx * SHARD) // BLK
     )
-    mask_rows = dot(pick.astype(BF16), block_mask[...].astype(BF16)).astype(BF16)
+    mask_rows = dot(pick.astype(BF16), mask_in[...].astype(BF16)).astype(BF16)
 
     def bias_step(step, carry):
         cols = pl.ds(pl.multiple_of(step * CHUNK, CHUNK), CHUNK)
@@ -154,36 +201,15 @@
         return carry
 
     lax.fori_loop(0, TOK // CHUNK, bias_step, 0)
-    query = stacked(queries[...])
-    grad = stacked(out_grad[...])
-    delta = jnp.sum(grad.astype(F32) * stacked(outputs[...]).astype(F32), axis=1, keepdims=True)
+    query = stacked(query_in[...])
+    grad = stacked(grad_in[...])
+    delta = jnp.sum(grad.astype(F32) * stacked(out_in[...]).astype(F32), axis=1, keepdims=True)
 
     for dz in (1, 3, 2):
         kv_gather.wait(dz, 0)
         kv_gather.along_y(dz)
         to_sibling(dz, 0)
 
-    act_first = slots(16)
-    act_sib = slots(16)
-
-    def act_shard(dzh, dx):
-        index = ((zh - dzh) % 4) * 8 + ((x - dx) % 4) * 2 + core
-        return act.at[pl.ds(pl.multiple_of(index * 64, 64), 64)]
-
-    def act_from_sibling(dzh, dx):
-        index = ((zh - dzh) % 4) * 8 + ((x - dx) % 4) * 2 + sib
-        return act.at[pl.ds(pl.multiple_of(index * 64, 64), 64)]
-
-    def act_along_x(dzh):
-        for dx in (1, 3, 2):
-            send(act_shard(dzh, 0), act_shard(dzh, 0), act_first + dzh * 4 + dx, at(dx=dx))
-        act_to_sibling(dzh, 0)
-
-    def act_to_sibling(dzh, dx):
-        send(act_shard(dzh, dx), act_shard(dzh, dx), act_sib + dzh * 4 + dx, at(dk=1))
-
-    for dzh in (1, 3, 2):
-        send(act_shard(0, 0), act_shard(0, 0), act_first + dzh * 4, at(dzh=dzh))
     act_along_x(0)
 
     for dz in range(4):
@@ -253,6 +279,12 @@
     q_all[:HD, own_lanes] = query_grad[:SHARD].T.astype(BF16)
     q_all[HD:, own_lanes] = query_grad[SHARD:].T.astype(BF16)
 
+    for dzh in (1, 3, 2):
+        @pl.when(rank < ranks[dzh])
+        def _(dzh=dzh):
+            pl.semaphore_wait(ready_sem.at[4 - dzh], 1)
+            act_along_z(dzh).start()
+
     arrive(sib_recv, core_slot)
     y_slot = slots(4)
     for dy in (1, 3, 2):
@@ -313,7 +345,7 @@
     g_all[:, own_lanes] = kv_sum.astype(BF16)
     g_gather = Gather(lambda index: g_all.at[:, lanes_of(index)])
     g_gather.start()
-    kv_out[...] = kv_sum.T.astype(BF16)
+    kv_out[...] = kv_sum.astype(BF16)
 
     for dzh in range(4):
         for dx in (1, 3, 2):
@@ -335,27 +367,37 @@
     for dz in range(4):
         for dy in (1, 3, 2):
             g_gather.wait(dz, dy)
-    wkv_out[...] = dot(g_all[...], act[...]).T.astype(BF16)
+    wkv_out[...] = dot(g_all[...], act[...]).astype(BF16)
 
     for item in sends:
         item.wait_send()
+
+
+def deliver(*refs):
+    for source, result in zip(refs[:4], refs[4:]):
+        result[...] = source[...]
 
 
 def per_device(inputs, queries, keys, values, outputs, out_grad, block_mask):
     vmem = pl.BlockSpec(memory_space=pltpu.VMEM)
     anywhere = pl.BlockSpec(memory_space=pl.ANY)
-    return pl.pallas_call(
+    shapes = (
+        jax.ShapeDtypeStruct((SHARD, 256), BF16),
+        jax.ShapeDtypeStruct((64, SHARD), BF16),
+        jax.ShapeDtypeStruct((512, 256), BF16),
+        jax.ShapeDtypeStruct((64, 512), BF16),
+    )
+    results = pl.pallas_call(
         body,
         name="attention_backward",
-        out_shape=(
-            jax.ShapeDtypeStruct((SHARD, 256), BF16),
-            jax.ShapeDtypeStruct((SHARD, 64), BF16),
-            jax.ShapeDtypeStruct((512, 256), BF16),
-            jax.ShapeDtypeStruct((512, 64), BF16),
-        ),
-        in_specs=[anywhere, vmem, anywhere, anywhere, vmem, vmem, vmem],
+        out_shape=shapes,
+        in_specs=[anywhere] * 7,
         out_specs=(vmem, vmem, vmem, vmem),
         scratch_shapes=[
+            pltpu.VMEM((SHARD, 256), BF16),
+            pltpu.VMEM((SHARD, 256), BF16),
+            pltpu.VMEM((SHARD, 256), BF16),
+            pltpu.VMEM((32, 32), jnp.int32),
             pltpu.VMEM((TOK, 512), BF16),
             pltpu.VMEM((2, TOK, HD), BF16),
             pltpu.VMEM((256, TOK), BF16),
@@ -373,15 +415,25 @@
             pltpu.VMEM((8, 64, HD), BF16),
             pltpu.SemaphoreType.DMA((112,)),
             pltpu.SemaphoreType.DMA((112,)),
-            pltpu.SemaphoreType.DMA((3,)),
+            pltpu.SemaphoreType.DMA((7,)),
+            pltpu.SemaphoreType.REGULAR((4,)),
         ],
         compiler_params=pltpu.CompilerParams(
-            collective_id=0, has_side_effects=True, vmem_limit_bytes=48 << 20
+            collective_id=0, has_side_effects=True, vmem_limit_bytes=VMEM_LIMIT
         ),
         cost_estimate=pl.CostEstimate(
             flops=1_400_000_000, bytes_accessed=4 << 20, transcendentals=256 * TOK
         ),
     )(inputs, queries, keys, values, outputs, out_grad, block_mask)
+    q_grad, kv_turned, weight_q, weight_kv_turned = pl.pallas_call(
+        deliver,
+        name="deliver",
+        out_shape=shapes,
+        in_specs=[vmem] * 4,
+        out_specs=[vmem] * 4,
+        compiler_params=pltpu.CompilerParams(vmem_limit_bytes=VMEM_LIMIT),
+    )(*results)
+    return q_grad, kv_turned.T, weight_q, weight_kv_turned.T
 
 
 def solution(mesh):

time: 70.2 us -> 59.3 us (0.84)
  the two profiles are of different devices: /device:TPU:6 before, /device:TPU:128 now
where the time goes in v2:
time: 59.3 us; the launch traced here: 59.1 us
  Pallas kernels  58.5 us (99%)
  between operations  0.64 us (1%)
    pallas_call x1, Pallas kernels, per_device(): pl.pallas_call(body, name='attention_backward', out_shape=shapes, in_spec...  56.7 us
    pallas_call x1, Pallas kernels, per_device(): pl.pallas_call(deliver, name='deliver', out_shape=shapes, in_specs=[vmem]...  1.76 us

profile of v2, /device:TPU:128, one launch (start us, length us, event | category | flops | bytes accessed | tf_op | source)
XLA Modules:
  0.0 59.1 jit_solution(17620082945100159014)
XLA Ops:
  0.6 56.7 %attention_backward.1 = (bf16[128,256]{1,0:T(8,128)(2,1)}, bf16[64,128]{1,0:T(8,128)(2,1)}, bf16[512,256]{1,0:T(8,128)(2,1)}, bf16[64,512]{1,0:T(8,128)(2,1)}) custom-call(bf16[64,512]{1,0:T(8,128)(2,1)} %inputs.1, bf16[128,256]{1,0:T(8,128)(2,1)} %queries.1, bf16[128,1024]{1,0:T(8,128)(2,1)} %keys.1, bf16[128,1024]{1,0:T(8,128)(2,1)} %values.1, ...), custom_call_target="tpu_custom_call" | custom-call | flops 1400000000 | bytes 4194304 | tf_op jit(solution)/shard_map/attention_backward/pallas_call | solution.py:390
  57.4 1.8 %deliver.1 = (bf16[128,256]{1,0:T(8,128)(2,1)}, bf16[64,128]{1,0:T(8,128)(2,1)}, bf16[512,256]{1,0:T(8,128)(2,1)}, bf16[64,512]{1,0:T(8,128)(2,1)}) custom-call(bf16[128,256]{1,0:T(8,128)(2,1)} %get-tuple-element.12.refs_0_, bf16[64,128]{1,0:T(8,128)(2,1)} %get-tuple-element.13.refs_1_, bf16[512,256]{1,0:T(8,128)(2,1)} %get-tuple-element.14.refs_2_, ...), custom_call_target="tpu_custom_call" | custom-call | tf_op jit(solution)/shard_map/deliver/pallas_call | solution.py:428

commit v3 on v2

--- a/solution.py
+++ b/solution.py
@@ -18,14 +18,6 @@
 F32 = jnp.float32
 BF16 = jnp.bfloat16
 
-PEERS = (
-    [(d, 0, 0, 0, 0) for d in (1, 2, 3)]
-    + [(0, d, 0, 0, 0) for d in (1, 2, 3)]
-    + [(0, 0, 0, d, 0) for d in (1, 2, 3)]
-    + [(0, 0, 0, 0, 1)]
-)
-
-
 def dot(left, right):
     return lax.dot_general(left, right, (((1,), (0,)), ((), ())), preferred_element_type=F32)
 
@@ -42,7 +34,7 @@
     inputs, queries, keys, values, outputs, out_grad, block_mask,
     q_out, kv_out, wq_out, wkv_out,
     query_in, grad_in, out_in, mask_in,
-    act, kv_all, q_all, g_all, scores, probs, dsc, bias,
+    act, kv_all, q_all, g_all, scores, slopes, probs, dsc, bias, top,
     sib_send, sib_recv, own, y_send, y_recv, zx_send, zx_recv,
     send_sem, recv_sem, local_sem, ready_sem,
 ):
@@ -84,6 +76,9 @@
 
     def arrive(dst, slot):
         copy(dst, dst, slot, at(dk=1)).wait_recv()
+
+    def signal(sem, device):
+        pl.semaphore_signal(sem, inc=1, device_id=device, device_id_type=MESH)
 
     own_rows = pl.ds(pl.multiple_of(ctx * SHARD, SHARD), SHARD)
     own_cols = pl.ds(pl.multiple_of(group * HD, HD), HD)
@@ -100,24 +95,49 @@
     for item in loads:
         item.start()
 
-    barrier = pltpu.get_barrier_semaphore()
-    for offset in PEERS:
-        pl.semaphore_signal(barrier, inc=1, device_id=at(*offset), device_id_type=MESH)
-    for dz in (1, 2, 3):
-        pl.semaphore_signal(barrier, inc=1, device_id=flip(dz), device_id_type=MESH)
     def rank_of(index):
         return jnp.where(index < 2, index, 5 - index)
 
-    rank = rank_of(zh)
-    ranks = {dzh: rank_of((zh + dzh) % 4) for dzh in (1, 2, 3)}
-    for dzh in (1, 2, 3):
-        @pl.when(rank < ranks[dzh])
-        def _(dzh=dzh):
-            pl.semaphore_signal(barrier, inc=1, device_id=at(dzh=dzh), device_id_type=MESH)
+    barrier = pltpu.get_barrier_semaphore()
+    for offset in (1, 2, 3):
+        signal(barrier, at(dy=offset))
+        signal(barrier, at(dz=offset))
+    signal(barrier, at(dk=1))
+
+    rank_z, rank_x = rank_of(zh), rank_of(x)
+    pair_first = (x == 0) | (x == 3)
+    links = {}
+    for offset in (1, 2, 3):
+        links["z", offset] = (
+            rank_z < rank_of((zh + offset) % 4), at(dzh=offset), offset, 4 - offset
+        )
+        links["x", offset] = (
+            rank_x < rank_of((x + offset) % 4), at(dx=offset), 4 + offset, 8 - offset
+        )
+        links["f", offset] = (pair_first, flip(offset), 8 + offset, 12 - offset)
+
+    for first, device, _, _ in links.values():
+        @pl.when(first)
+        def _(device=device):
+            signal(barrier, device)
 
     for item in loads[:3]:
         item.wait()
-    pl.semaphore_wait(barrier, len(PEERS) + 3 + rank)
+    pl.semaphore_wait(barrier, 7 + rank_z + rank_x + jnp.where(pair_first, 0, 3))
+
+    def answer(key):
+        first, device, slot, _ = links[key]
+
+        @pl.when(jnp.logical_not(first))
+        def _():
+            signal(ready_sem.at[slot], device)
+
+    def await_answer(key):
+        first, _, _, slot = links[key]
+
+        @pl.when(first)
+        def _():
+            pl.semaphore_wait(ready_sem.at[slot], 1)
 
     class Gather:
         def __init__(self, place):
@@ -169,16 +189,28 @@
     def act_to_sibling(dzh, dx):
         send(act_shard(dzh, dx), act_shard(dzh, dx), act_sib + dzh * 4 + dx, at(dk=1))
 
-    def act_along_z(dzh):
-        return copy(act_shard(0, 0), act_shard(0, 0), act_first + dzh * 4, at(dzh=dzh))
-
+    act_z = {
+        dzh: copy(act_shard(0, 0), act_shard(0, 0), act_first + dzh * 4, at(dzh=dzh))
+        for dzh in (1, 3, 2)
+    }
+    sends.extend(act_z.values())
+
+    for key in links:
+        answer(key)
     for dzh in (1, 3, 2):
-        sends.append(act_along_z(dzh))
-
-        @pl.when(rank > ranks[dzh])
+        @pl.when(jnp.logical_not(links["z", dzh][0]))
         def _(dzh=dzh):
-            pl.semaphore_signal(ready_sem.at[dzh], inc=1, device_id=at(dzh=dzh), device_id_type=MESH)
-            act_along_z(dzh).start()
+            act_z[dzh].start()
+
+    def act_z_later(pairs):
+        for dzh in (1, 3, 2):
+            first, _, _, slot = links["z", dzh]
+            farthest = (zh == 0) & (dzh == 2)
+
+            @pl.when(first & (farthest if pairs == "far" else jnp.logical_not(farthest)))
+            def _(dzh=dzh, slot=slot):
+                pl.semaphore_wait(ready_sem.at[slot], 1)
+                act_z[dzh].start()
 
     for item in loads[3:]:
         item.wait()
@@ -205,40 +237,48 @@
     grad = stacked(grad_in[...])
     delta = jnp.sum(grad.astype(F32) * stacked(out_in[...]).astype(F32), axis=1, keepdims=True)
 
+    def block_scores(dz, dy):
+        index = ((z - dz) % 4) * 4 + (y - dy) % 4
+        if dz or dy:
+            arrive(kv_all.at[sib, rows_of(index)], sib_first + dz * 4 + dy)
+        cols = pl.ds(pl.multiple_of(index * SHARD, SHARD), SHARD)
+        part = dot_t(query, kv_all[0, rows_of(index), :]) + bias[:, cols]
+        scores[:, cols] = part
+        slopes[:, cols] = dot_t(grad, kv_all[1, rows_of(index), :])
+        top[...] = jnp.maximum(top[...], part) if dz or dy else part
+
+    block_scores(0, 0)
+
     for dz in (1, 3, 2):
         kv_gather.wait(dz, 0)
         kv_gather.along_y(dz)
         to_sibling(dz, 0)
-
+    for dx in (1, 3, 2):
+        await_answer(("x", dx))
     act_along_x(0)
 
-    for dz in range(4):
+    waiting = [(1, 0), (3, 0), (2, 0)]
+    for dz in (0, 1, 3, 2):
         for dy in (1, 3, 2):
             kv_gather.wait(dz, dy)
             to_sibling(dz, dy)
-    for dz in range(4):
-        for dy in range(4):
-            if dz or dy:
-                index = ((z - dz) % 4) * 4 + (y - dy) % 4
-                arrive(kv_all.at[sib, rows_of(index)], sib_first + dz * 4 + dy)
+            waiting.append((dz, dy))
+            if len(waiting) > 2:
+                block_scores(*waiting.pop(0))
+        if dz == 1:
+            act_z_later("near")
+    for block in waiting:
+        block_scores(*block)
 
     scale = HD ** -0.5
-
-    def score_step(step, top):
-        cols = pl.ds(pl.multiple_of(step * CHUNK, CHUNK), CHUNK)
-        part = dot_t(query, kv_all[0, cols, :]) * scale + bias[:, cols]
-        scores[:, cols] = part
-        return jnp.maximum(top, jnp.maximum(part[:, :HD], part[:, HD:]))
-
-    top = lax.fori_loop(0, TOK // CHUNK, score_step, jnp.full((2 * SHARD, HD), NEG, F32))
-    row_max = jnp.max(top, axis=1, keepdims=True)
+    power = scale * 1.4426950408889634
+    row_max = jnp.max(top[...], axis=1, keepdims=True)
 
     def prob_step(step, total):
         cols = pl.ds(pl.multiple_of(step * CHUNK, CHUNK), CHUNK)
-        part = jnp.exp(scores[:, cols] - row_max)
-        slope = dot_t(grad, kv_all[1, cols, :])
+        part = jnp.exp2((scores[:, cols] - row_max) * power)
         probs[:, cols] = part.astype(BF16)
-        dsc[:, cols] = (part * (slope - delta)).astype(BF16)
+        dsc[:, cols] = (part * (slopes[:, cols] - delta)).astype(BF16)
         return total + part[:, :HD] + part[:, HD:]
 
     total = lax.fori_loop(0, TOK // CHUNK, prob_step, jnp.zeros((2 * SHARD, HD), F32))
@@ -254,23 +294,37 @@
     query_t = mine_first(query.astype(F32) * (inverse * scale))
     grad_t = mine_first(grad.astype(F32) * inverse)
 
-    def term_step(step, carry):
-        cols = pl.ds(pl.multiple_of(step * CHUNK, CHUNK), CHUNK)
-        key_part = dot(query_t, dsc[:, cols])
-        value_part = dot(grad_t, probs[:, cols])
-        for half in range(2):
-            index = step * 2 + half
-            block = (index % 4) * 4 + index // 4
-            lanes = slice(half * HD, (half + 1) * HD)
-            own[block, 0] = key_part[:64, lanes]
-            own[block, 1] = value_part[:64, lanes]
-            sib_send[block, 0] = key_part[64:, lanes].astype(BF16)
-            sib_send[block, 1] = value_part[64:, lanes].astype(BF16)
-        return carry
-
-    lax.fori_loop(0, TOK // CHUNK, term_step, 0)
-    core_slot = slots(1)
-    send(sib_send, sib_recv, core_slot, at(dk=1))
+    core_slot = slots(4)
+    y_slot = slots(4)
+
+    def terms(dy):
+        def term_step(step, carry):
+            index = step * 4 + (y + dy) % 4
+            cols = pl.ds(pl.multiple_of(index * SHARD, SHARD), SHARD)
+            key_part = dot(query_t, dsc[:, cols])
+            value_part = dot(grad_t, probs[:, cols])
+            own[dy, step, 0] = key_part[:64]
+            own[dy, step, 1] = value_part[:64]
+            sib_send[dy, step, 0] = key_part[64:].astype(BF16)
+            sib_send[dy, step, 1] = value_part[64:].astype(BF16)
+            return carry
+
+        lax.fori_loop(0, 4, term_step, 0)
+        send(sib_send.at[dy], sib_recv.at[dy], core_slot + dy, at(dk=1))
+
+    def to_y(dy):
+        arrive(sib_recv.at[dy], core_slot + dy)
+        y_send[dy - 1] = (own[dy] + sib_recv[dy].astype(F32)).astype(BF16)
+        send(y_send.at[dy - 1], y_recv.at[dy - 1], y_slot + dy, at(dy=dy))
+
+    terms(2)
+    terms(1)
+    to_y(2)
+    terms(3)
+    to_y(1)
+    terms(0)
+    to_y(3)
+    act_z_later("far")
 
     query_grad = dot(dsc[...], kv_all[0]) * (inverse * scale)
     q_out[:, :HD] = query_grad[:SHARD].astype(BF16)
@@ -279,50 +333,28 @@
     q_all[:HD, own_lanes] = query_grad[:SHARD].T.astype(BF16)
     q_all[HD:, own_lanes] = query_grad[SHARD:].T.astype(BF16)
 
-    for dzh in (1, 3, 2):
-        @pl.when(rank < ranks[dzh])
-        def _(dzh=dzh):
-            pl.semaphore_wait(ready_sem.at[4 - dzh], 1)
-            act_along_z(dzh).start()
-
-    arrive(sib_recv, core_slot)
-    y_slot = slots(4)
-    for dy in (1, 3, 2):
-        dest = (y + dy) % 4
-
-        def add_step(step, carry):
-            block = dest * 4 + step
-            y_send[dy - 1, step] = (own[block] + sib_recv[block].astype(F32)).astype(BF16)
-            return carry
-
-        lax.fori_loop(0, 4, add_step, 0)
-        send(y_send.at[dy - 1], y_recv.at[dy - 1], y_slot + dy, at(dy=dy))
-
     def lanes_of(index):
         return pl.ds(pl.multiple_of(index * SHARD, SHARD), SHARD)
 
     q_gather = Gather(lambda index: q_all.at[:, lanes_of(index)])
     q_gather.start()
 
-    for dzh in (1, 3, 2):
+    for dzh in (1, 3):
         arrive(act_shard(dzh, 0), act_first + dzh * 4)
         act_along_x(dzh)
 
+    arrive(sib_recv.at[0], core_slot)
     for dy in (1, 3, 2):
         arrive(y_recv.at[dy - 1], y_slot + dy)
-
-    def y_sum(step, carry):
-        block = y * 4 + step
-        value = own[block] + sib_recv[block].astype(F32)
-        for dy in (1, 2, 3):
-            value = value + y_recv[dy - 1, step].astype(F32)
-        own[block] = value
-        zx_send[step] = value.astype(BF16)
-        return carry
-
-    lax.fori_loop(0, 4, y_sum, 0)
+    y_sum = own[0] + sib_recv[0].astype(F32)
+    for dy in (1, 2, 3):
+        y_sum = y_sum + y_recv[dy - 1].astype(F32)
+    own[0] = y_sum
+    zx_send[...] = y_sum.astype(BF16)
 
     zx_slot = slots(8)
+    for dz in (1, 2, 3):
+        await_answer(("f", dz))
     for dz in (1, 3, 2, 0):
         for dx in (0, 1):
             if dz or dx:
@@ -336,8 +368,10 @@
     for dz in (1, 3, 2):
         q_gather.wait(dz, 0)
         q_gather.along_y(dz)
-
-    kv_sum = own[y * 4 + z, side]
+    arrive(act_shard(2, 0), act_first + 8)
+    act_along_x(2)
+
+    kv_sum = own[0, z, side]
     for slot in range(1, 8):
         arrive(zx_recv.at[slot], zx_slot + slot)
     for slot in range(1, 8):
@@ -347,7 +381,7 @@
     g_gather.start()
     kv_out[...] = kv_sum.astype(BF16)
 
-    for dzh in range(4):
+    for dzh in (0, 1, 3):
         for dx in (1, 3, 2):
             arrive(act_shard(dzh, dx), act_first + dzh * 4 + dx)
             act_to_sibling(dzh, dx)
@@ -356,6 +390,9 @@
         g_gather.wait(dz, 0)
         g_gather.along_y(dz)
 
+    for dx in (1, 3, 2):
+        arrive(act_shard(2, dx), act_first + 8 + dx)
+        act_to_sibling(2, dx)
     for dz in range(4):
         for dy in (1, 3, 2):
             q_gather.wait(dz, dy)
@@ -403,20 +440,22 @@
             pltpu.VMEM((256, TOK), BF16),
             pltpu.VMEM((64, TOK), BF16),
             pltpu.VMEM((256, TOK), F32),
+            pltpu.VMEM((256, TOK), F32),
             pltpu.VMEM((256, TOK), BF16),
             pltpu.VMEM((256, TOK), BF16),
             pltpu.VMEM((256, TOK), F32),
-            pltpu.VMEM((16, 2, 64, HD), BF16),
-            pltpu.VMEM((16, 2, 64, HD), BF16),
-            pltpu.VMEM((16, 2, 64, HD), F32),
+            pltpu.VMEM((256, HD), F32),
+            pltpu.VMEM((4, 4, 2, 64, HD), BF16),
+            pltpu.VMEM((4, 4, 2, 64, HD), BF16),
+            pltpu.VMEM((4, 4, 2, 64, HD), F32),
             pltpu.VMEM((3, 4, 2, 64, HD), BF16),
             pltpu.VMEM((3, 4, 2, 64, HD), BF16),
             pltpu.VMEM((4, 2, 64, HD), BF16),
             pltpu.VMEM((8, 64, HD), BF16),
-            pltpu.SemaphoreType.DMA((112,)),
-            pltpu.SemaphoreType.DMA((112,)),
+            pltpu.SemaphoreType.DMA((128,)),
+            pltpu.SemaphoreType.DMA((128,)),
             pltpu.SemaphoreType.DMA((7,)),
-            pltpu.SemaphoreType.REGULAR((4,)),
+            pltpu.SemaphoreType.REGULAR((12,)),
         ],
         compiler_params=pltpu.CompilerParams(
             collective_id=0, has_side_effects=True, vmem_limit_bytes=VMEM_LIMIT

time: 59.3 us -> 54.6 us (0.921)
  the two profiles are of different devices: /device:TPU:128 before, /device:TPU:6 now
where the time goes in v3:
time: 54.6 us; the launch traced here: 53.7 us
  Pallas kernels  53 us (97%)
  between operations  0.64 us (1%)
    pallas_call x1, Pallas kernels, per_device(): pl.pallas_call(body, name='attention_backward', out_shape=shapes, in_spec...  51.3 us
    pallas_call x1, Pallas kernels, per_device(): pl.pallas_call(deliver, name='deliver', out_shape=shapes, in_specs=[vmem]...  1.76 us

profile of v3, /device:TPU:6, one launch (start us, length us, event | category | flops | bytes accessed | tf_op | source)
XLA Modules:
  0.0 53.7 jit_solution(15033418647407488437)
XLA Ops:
  0.6 51.3 %attention_backward.1 = (bf16[128,256]{1,0:T(8,128)(2,1)}, bf16[64,128]{1,0:T(8,128)(2,1)}, bf16[512,256]{1,0:T(8,128)(2,1)}, bf16[64,512]{1,0:T(8,128)(2,1)}) custom-call(bf16[64,512]{1,0:T(8,128)(2,1)} %inputs.1, bf16[128,256]{1,0:T(8,128)(2,1)} %queries.1, bf16[128,1024]{1,0:T(8,128)(2,1)} %keys.1, bf16[128,1024]{1,0:T(8,128)(2,1)} %values.1, ...), custom_call_target="tpu_custom_call" | custom-call | flops 1400000000 | bytes 4194304 | tf_op jit(solution)/shard_map/attention_backward/pallas_call | solution.py:427
  51.9 1.8 %deliver.1 = (bf16[128,256]{1,0:T(8,128)(2,1)}, bf16[64,128]{1,0:T(8,128)(2,1)}, bf16[512,256]{1,0:T(8,128)(2,1)}, bf16[64,512]{1,0:T(8,128)(2,1)}) custom-call(bf16[128,256]{1,0:T(8,128)(2,1)} %get-tuple-element.12.refs_0_, bf16[64,128]{1,0:T(8,128)(2,1)} %get-tuple-element.13.refs_1_, bf16[512,256]{1,0:T(8,128)(2,1)} %get-tuple-element.14.refs_2_, ...), custom_call_target="tpu_custom_call" | custom-call | tf_op jit(solution)/shard_map/deliver/pallas_call | solution.py:467

commit v4 on v3

--- a/solution.py
+++ b/solution.py
@@ -11,7 +11,7 @@
 BLK = 64
 TOK = 2048
 SHARD = 128
-CHUNK = 256
+SPAN = 512
 MESH = pl.DeviceIdType.MESH
 NEG = -1e30
 VMEM_LIMIT = 60 << 20
@@ -34,7 +34,7 @@
     inputs, queries, keys, values, outputs, out_grad, block_mask,
     q_out, kv_out, wq_out, wkv_out,
     query_in, grad_in, out_in, mask_in,
-    act, kv_all, q_all, g_all, scores, slopes, probs, dsc, bias, top,
+    act, kv_all, q_all, g_all, scores, slopes, probs, dsc, bias, top, query_turned, grad_turned,
     sib_send, sib_recv, own, y_send, y_recv, zx_send, zx_recv,
     send_sem, recv_sem, local_sem, ready_sem,
 ):
@@ -80,7 +80,10 @@
     def signal(sem, device):
         pl.semaphore_signal(sem, inc=1, device_id=device, device_id_type=MESH)
 
-    own_rows = pl.ds(pl.multiple_of(ctx * SHARD, SHARD), SHARD)
+    def place_of(dz, dy):
+        return pl.ds(pl.multiple_of((((y - dy) % 4) * 4 + (z - dz) % 4) * SHARD, SHARD), SHARD)
+
+    own_rows = place_of(0, 0)
     own_cols = pl.ds(pl.multiple_of(group * HD, HD), HD)
     own_act = pl.ds(pl.multiple_of(head * 64, 64), 64)
     loads = [
@@ -140,12 +143,9 @@
             pl.semaphore_wait(ready_sem.at[slot], 1)
 
     class Gather:
-        def __init__(self, place):
-            self.place = place
+        def __init__(self, shard):
+            self.shard = shard
             self.first = slots(16)
-
-        def shard(self, dz, dy):
-            return self.place(((z - dz) % 4) * 4 + (y - dy) % 4)
 
         def start(self):
             for dz in (1, 3, 2):
@@ -159,10 +159,7 @@
         def wait(self, dz, dy):
             arrive(self.shard(dz, dy), self.first + dz * 4 + dy)
 
-    def rows_of(index):
-        return pl.ds(pl.multiple_of(index * SHARD, SHARD), SHARD)
-
-    kv_gather = Gather(lambda index: kv_all.at[core, rows_of(index)])
+    kv_gather = Gather(lambda dz, dy: kv_all.at[core, place_of(dz, dy)])
     kv_gather.start()
     sib_first = slots(16)
 
@@ -197,10 +194,16 @@
 
     for key in links:
         answer(key)
-    for dzh in (1, 3, 2):
-        @pl.when(jnp.logical_not(links["z", dzh][0]))
-        def _(dzh=dzh):
-            act_z[dzh].start()
+    def act_z_lower(to_first):
+        for dzh in (1, 3, 2):
+            first_rank = (zh + dzh) % 4 == 0
+            chosen = first_rank if to_first else jnp.logical_not(first_rank)
+
+            @pl.when(jnp.logical_not(links["z", dzh][0]) & chosen)
+            def _(dzh=dzh):
+                act_z[dzh].start()
+
+    act_z_lower(True)
 
     def act_z_later(pairs):
         for dzh in (1, 3, 2):
@@ -214,7 +217,7 @@
 
     for item in loads[3:]:
         item.wait()
-    row_ids = lax.broadcasted_iota(jnp.int32, (2 * SHARD, CHUNK), 0) % SHARD + ctx * SHARD
+    row_ids = lax.broadcasted_iota(jnp.int32, (2 * SHARD, SHARD), 0) % SHARD + ctx * SHARD
     pick = (
         lax.broadcasted_iota(jnp.int32, (2 * SHARD, 32), 1)
         == (lax.broadcasted_iota(jnp.int32, (2 * SHARD, 32), 0) % SHARD + ctx * SHARD) // BLK
@@ -222,29 +225,39 @@
     mask_rows = dot(pick.astype(BF16), mask_in[...].astype(BF16)).astype(BF16)
 
     def bias_step(step, carry):
-        cols = pl.ds(pl.multiple_of(step * CHUNK, CHUNK), CHUNK)
-        col_ids = lax.broadcasted_iota(jnp.int32, (2 * SHARD, CHUNK), 1) + step * CHUNK
+        cols = pl.ds(pl.multiple_of(step * SHARD, SHARD), SHARD)
+        first = ((step % 4) * 4 + step // 4) * SHARD
+        col_ids = lax.broadcasted_iota(jnp.int32, (2 * SHARD, SHARD), 1) + first
         spread = (
-            (lax.broadcasted_iota(jnp.int32, (32, CHUNK), 1) + step * CHUNK) // BLK
-            == lax.broadcasted_iota(jnp.int32, (32, CHUNK), 0)
+            (lax.broadcasted_iota(jnp.int32, (32, SHARD), 1) + first) // BLK
+            == lax.broadcasted_iota(jnp.int32, (32, SHARD), 0)
         )
         wide = dot(mask_rows, spread.astype(BF16))
         bias[:, cols] = jnp.where((wide > 0.5) & (col_ids <= row_ids), 0.0, NEG)
         return carry
 
-    lax.fori_loop(0, TOK // CHUNK, bias_step, 0)
+    lax.fori_loop(0, TOK // SHARD, bias_step, 0, unroll=2)
     query = stacked(query_in[...])
     grad = stacked(grad_in[...])
     delta = jnp.sum(grad.astype(F32) * stacked(out_in[...]).astype(F32), axis=1, keepdims=True)
 
+    def mine_first(value):
+        turned = value.astype(F32).T
+        low, high = turned[:64], turned[64:]
+        return jnp.concatenate(
+            [jnp.where(core == 0, low, high), jnp.where(core == 0, high, low)], axis=0
+        )
+
+    query_turned[...] = mine_first(query)
+    grad_turned[...] = mine_first(grad)
+
     def block_scores(dz, dy):
-        index = ((z - dz) % 4) * 4 + (y - dy) % 4
+        span = place_of(dz, dy)
         if dz or dy:
-            arrive(kv_all.at[sib, rows_of(index)], sib_first + dz * 4 + dy)
-        cols = pl.ds(pl.multiple_of(index * SHARD, SHARD), SHARD)
-        part = dot_t(query, kv_all[0, rows_of(index), :]) + bias[:, cols]
-        scores[:, cols] = part
-        slopes[:, cols] = dot_t(grad, kv_all[1, rows_of(index), :])
+            arrive(kv_all.at[sib, span], sib_first + dz * 4 + dy)
+        part = dot_t(query, kv_all[0, span, :]) + bias[:, span]
+        scores[:, span] = part
+        slopes[:, span] = dot_t(grad, kv_all[1, span, :])
         top[...] = jnp.maximum(top[...], part) if dz or dy else part
 
     block_scores(0, 0)
@@ -253,6 +266,7 @@
         kv_gather.wait(dz, 0)
         kv_gather.along_y(dz)
         to_sibling(dz, 0)
+    act_z_lower(False)
     for dx in (1, 3, 2):
         await_answer(("x", dx))
     act_along_x(0)
@@ -273,59 +287,60 @@
     scale = HD ** -0.5
     power = scale * 1.4426950408889634
     row_max = jnp.max(top[...], axis=1, keepdims=True)
-
-    def prob_step(step, total):
-        cols = pl.ds(pl.multiple_of(step * CHUNK, CHUNK), CHUNK)
+    total = jnp.zeros((2 * SHARD, HD), F32)
+    for step in range(TOK // SPAN):
+        cols = slice(step * SPAN, (step + 1) * SPAN)
         part = jnp.exp2((scores[:, cols] - row_max) * power)
+        scores[:, cols] = part
         probs[:, cols] = part.astype(BF16)
-        dsc[:, cols] = (part * (slopes[:, cols] - delta)).astype(BF16)
-        return total + part[:, :HD] + part[:, HD:]
-
-    total = lax.fori_loop(0, TOK // CHUNK, prob_step, jnp.zeros((2 * SHARD, HD), F32))
+        for lane in range(0, SPAN, HD):
+            total = total + part[:, lane : lane + HD]
+    inverse_row = 1.0 / jnp.sum(total.T, axis=0, keepdims=True)
+    query_t = (query_turned[...] * (inverse_row * scale)).astype(BF16)
+    grad_t = (grad_turned[...] * inverse_row).astype(BF16)
+
+    core_slot = slots(8)
+    y_slot = slots(8)
+
+    def span_of(dy):
+        return pl.ds(pl.multiple_of(((y + dy) % 4) * SPAN, SPAN), SPAN)
+
+    def terms(part, dy):
+        span = span_of(dy)
+        if part:
+            result = dot(grad_t, probs[:, span])
+        else:
+            slope = (scores[:, span] * (slopes[:, span] - delta)).astype(BF16)
+            dsc[:, span] = slope
+            result = dot(query_t, slope)
+        for step in range(4):
+            lanes = slice(step * SHARD, (step + 1) * SHARD)
+            own[part, dy, step] = result[:64, lanes]
+            sib_send[part, dy, step] = result[64:, lanes].astype(BF16)
+        send(sib_send.at[part, dy], sib_recv.at[part, dy], core_slot + part * 4 + dy, at(dk=1))
+
+    def to_y(part, dy):
+        arrive(sib_recv.at[part, dy], core_slot + part * 4 + dy)
+        y_send[part, dy - 1] = (own[part, dy] + sib_recv[part, dy].astype(F32)).astype(BF16)
+        send(
+            y_send.at[part, dy - 1], y_recv.at[part, dy - 1], y_slot + part * 4 + dy, at(dy=dy)
+        )
+
+    for dy in (2, 1, 3, 0):
+        terms(1, dy)
+    terms(0, 2)
+    to_y(1, 2)
+    to_y(1, 1)
+    terms(0, 1)
+    to_y(1, 3)
+    terms(0, 3)
+    to_y(0, 2)
+    terms(0, 0)
+    to_y(0, 1)
+    to_y(0, 3)
+    act_z_later("far")
+
     inverse = 1.0 / jnp.sum(total, axis=1, keepdims=True)
-
-    def mine_first(value):
-        turned = value.T
-        low, high = turned[:64], turned[64:]
-        return jnp.concatenate(
-            [jnp.where(core == 0, low, high), jnp.where(core == 0, high, low)], axis=0
-        ).astype(BF16)
-
-    query_t = mine_first(query.astype(F32) * (inverse * scale))
-    grad_t = mine_first(grad.astype(F32) * inverse)
-
-    core_slot = slots(4)
-    y_slot = slots(4)
-
-    def terms(dy):
-        def term_step(step, carry):
-            index = step * 4 + (y + dy) % 4
-            cols = pl.ds(pl.multiple_of(index * SHARD, SHARD), SHARD)
-            key_part = dot(query_t, dsc[:, cols])
-            value_part = dot(grad_t, probs[:, cols])
-            own[dy, step, 0] = key_part[:64]
-            own[dy, step, 1] = value_part[:64]
-            sib_send[dy, step, 0] = key_part[64:].astype(BF16)
-            sib_send[dy, step, 1] = value_part[64:].astype(BF16)
-            return carry
-
-        lax.fori_loop(0, 4, term_step, 0)
-        send(sib_send.at[dy], sib_recv.at[dy], core_slot + dy, at(dk=1))
-
-    def to_y(dy):
-        arrive(sib_recv.at[dy], core_slot + dy)
-        y_send[dy - 1] = (own[dy] + sib_recv[dy].astype(F32)).astype(BF16)
-        send(y_send.at[dy - 1], y_recv.at[dy - 1], y_slot + dy, at(dy=dy))
-
-    terms(2)
-    terms(1)
-    to_y(2)
-    terms(3)
-    to_y(1)
-    terms(0)
-    to_y(3)
-    act_z_later("far")
-
     query_grad = dot(dsc[...], kv_all[0]) * (inverse * scale)
     q_out[:, :HD] = query_grad[:SHARD].astype(BF16)
     q_out[:, HD:] = query_grad[SHARD:].astype(BF16)
@@ -333,37 +348,43 @@
     q_all[:HD, own_lanes] = query_grad[:SHARD].T.astype(BF16)
     q_all[HD:, own_lanes] = query_grad[SHARD:].T.astype(BF16)
 
-    def lanes_of(index):
+    def lanes_of(dz, dy):
+        index = ((z - dz) % 4) * 4 + (y - dy) % 4
         return pl.ds(pl.multiple_of(index * SHARD, SHARD), SHARD)
 
-    q_gather = Gather(lambda index: q_all.at[:, lanes_of(index)])
+    q_gather = Gather(lambda dz, dy: q_all.at[:, lanes_of(dz, dy)])
     q_gather.start()
 
     for dzh in (1, 3):
         arrive(act_shard(dzh, 0), act_first + dzh * 4)
         act_along_x(dzh)
 
-    arrive(sib_recv.at[0], core_slot)
-    for dy in (1, 3, 2):
-        arrive(y_recv.at[dy - 1], y_slot + dy)
-    y_sum = own[0] + sib_recv[0].astype(F32)
-    for dy in (1, 2, 3):
-        y_sum = y_sum + y_recv[dy - 1].astype(F32)
-    own[0] = y_sum
-    zx_send[...] = y_sum.astype(BF16)
-
     zx_slot = slots(8)
+
+    def to_zx(part):
+        arrive(sib_recv.at[part, 0], core_slot + part * 4)
+        for dy in (1, 3, 2):
+            arrive(y_recv.at[part, dy - 1], y_slot + part * 4 + dy)
+        y_sum = own[part, 0] + sib_recv[part, 0].astype(F32)
+        for dy in (1, 2, 3):
+            y_sum = y_sum + y_recv[part, dy - 1].astype(F32)
+        own[part, 0] = y_sum
+        zx_send[part] = y_sum.astype(BF16)
+        other = jnp.where(side == part, 0, 1)
+        for dz in (1, 3, 2):
+            slot = dz * 2 + other
+            device = (((z + dz) % 4) * 4 + y, zh * 8 + (x - side + part) * 2 + core)
+            send(zx_send.at[part, (z + dz) % 4], zx_recv.at[slot], zx_slot + slot, device)
+
+        @pl.when(side != part)
+        def _():
+            copy(zx_send.at[part, z], zx_recv.at[1], zx_slot + 1, flip(0)).start()
+
     for dz in (1, 2, 3):
         await_answer(("f", dz))
-    for dz in (1, 3, 2, 0):
-        for dx in (0, 1):
-            if dz or dx:
-                part = side if dx == 0 else 1 - side
-                slot = dz * 2 + dx
-                send(
-                    zx_send.at[(z + dz) % 4, part], zx_recv.at[slot], zx_slot + slot,
-                    flip(dz) if dx else at(dz=dz),
-                )
+    to_zx(1)
+    to_zx(0)
+    sends.append(copy(zx_send.at[0, 0], zx_recv.at[1], zx_slot + 1, flip(0)))
 
     for dz in (1, 3, 2):
         q_gather.wait(dz, 0)
@@ -371,13 +392,13 @@
     arrive(act_shard(2, 0), act_first + 8)
     act_along_x(2)
 
-    kv_sum = own[0, z, side]
+    kv_sum = own[side, 0, z]
     for slot in range(1, 8):
         arrive(zx_recv.at[slot], zx_slot + slot)
     for slot in range(1, 8):
         kv_sum = kv_sum + zx_recv[slot].astype(F32)
     g_all[:, own_lanes] = kv_sum.astype(BF16)
-    g_gather = Gather(lambda index: g_all.at[:, lanes_of(index)])
+    g_gather = Gather(lambda dz, dy: g_all.at[:, lanes_of(dz, dy)])
     g_gather.start()
     kv_out[...] = kv_sum.astype(BF16)
 
@@ -411,8 +432,15 @@
 
 
 def deliver(*refs):
-    for source, result in zip(refs[:4], refs[4:]):
-        result[...] = source[...]
+    sources, results, sem = refs[:4], refs[4:8], refs[8]
+    items = [
+        pltpu.make_async_copy(source, result, sem.at[index])
+        for index, (source, result) in enumerate(zip(sources, results))
+    ]
+    for item in items:
+        item.start()
+    for item in items:
+        item.wait()
 
 
 def per_device(inputs, queries, keys, values, outputs, out_grad, block_mask):
@@ -427,7 +455,7 @@
     results = pl.pallas_call(
         body,
         name="attention_backward",
-        out_shape=shapes,
+        out_shape=tuple(pltpu.VMEM(shape.shape, shape.dtype) for shape in shapes),
         in_specs=[anywhere] * 7,
         out_specs=(vmem, vmem, vmem, vmem),
         scratch_shapes=[
@@ -445,12 +473,14 @@
             pltpu.VMEM((256, TOK), BF16),
             pltpu.VMEM((256, TOK), F32),
             pltpu.VMEM((256, HD), F32),
-            pltpu.VMEM((4, 4, 2, 64, HD), BF16),
-            pltpu.VMEM((4, 4, 2, 64, HD), BF16),
-            pltpu.VMEM((4, 4, 2, 64, HD), F32),
-            pltpu.VMEM((3, 4, 2, 64, HD), BF16),
-            pltpu.VMEM((3, 4, 2, 64, HD), BF16),
-            pltpu.VMEM((4, 2, 64, HD), BF16),
+            pltpu.VMEM((HD, 256), F32),
+            pltpu.VMEM((HD, 256), F32),
+            pltpu.VMEM((2, 4, 4, 64, HD), BF16),
+            pltpu.VMEM((2, 4, 4, 64, HD), BF16),
+            pltpu.VMEM((2, 4, 4, 64, HD), F32),
+            pltpu.VMEM((2, 3, 4, 64, HD), BF16),
+            pltpu.VMEM((2, 3, 4, 64, HD), BF16),
+            pltpu.VMEM((2, 4, 64, HD), BF16),
             pltpu.VMEM((8, 64, HD), BF16),
             pltpu.SemaphoreType.DMA((128,)),
             pltpu.SemaphoreType.DMA((128,)),
@@ -469,8 +499,9 @@
         name="deliver",
         out_shape=shapes,
         in_specs=[vmem] * 4,
-        out_specs=[vmem] * 4,
-        compiler_params=pltpu.CompilerParams(vmem_limit_bytes=VMEM_LIMIT),
+        out_specs=[anywhere] * 4,
+        scratch_shapes=[pltpu.SemaphoreType.DMA((4,))],
+        compiler_params=pltpu.CompilerParams(vmem_limit_bytes=4 << 20),
     )(*results)
     return q_grad, kv_turned.T, weight_q, weight_kv_turned.T
 

time: 54.6 us -> 50.7 us (0.929)
  Pallas kernels: 53 us -> 49.5 us
    pallas_call x1, Pallas kernels: 51.3 us -> 48.7 us  [per_device(): pl.pallas_call(body, name='attention_backward', out_shape=tuple((pltpu.VM...]
    pallas_call x1, Pallas kernels: 1.76 us -> 0.78 us  [per_device(): pl.pallas_call(deliver, name='deliver', out_shape=shapes, in_specs=[vmem]...]
where the time goes in v4:
time: 50.7 us; the launch traced here: 50.2 us
  Pallas kernels  49.5 us (98%)
  between operations  0.64 us (1%)
    pallas_call x1, Pallas kernels, per_device(): pl.pallas_call(body, name='attention_backward', out_shape=tuple((pltpu.VM...  48.7 us

profile of v4, /device:TPU:6, one launch (start us, length us, event | category | flops | bytes accessed | tf_op | source)
XLA Modules:
  0.0 50.2 jit_solution(8251358222317784609)
XLA Ops:
  0.6 48.7 %attention_backward.1 = (bf16[128,256]{1,0:T(8,128)(2,1)S(1)}, bf16[64,128]{1,0:T(8,128)(2,1)S(1)}, bf16[512,256]{1,0:T(8,128)(2,1)S(1)}, bf16[64,512]{1,0:T(8,128)(2,1)S(1)}) custom-call(bf16[64,512]{1,0:T(8,128)(2,1)} %inputs.1, bf16[128,256]{1,0:T(8,128)(2,1)} %queries.1, bf16[128,1024]{1,0:T(8,128)(2,1)} %keys.1, bf16[128,1024]{1,0:T(8,128)(2,1)} %values.1, ...), custom_call_target="tpu_custom_call" | custom-call | flops 1400000000 | bytes 4194304 | tf_op jit(solution)/shard_map/attention_backward/pallas_call | solution.py:455
  49.4 0.8 %deliver.1 = (bf16[128,256]{1,0:T(8,128)(2,1)}, bf16[64,128]{1,0:T(8,128)(2,1)}, bf16[512,256]{1,0:T(8,128)(2,1)}, bf16[64,512]{1,0:T(8,128)(2,1)}) custom-call(bf16[128,256]{1,0:T(8,128)(2,1)S(1)} %get-tuple-element.12.refs_0_, bf16[64,128]{1,0:T(8,128)(2,1)S(1)} %get-tuple-element.13.refs_1_, bf16[512,256]{1,0:T(8,128)(2,1)S(1)} %get-tuple-element.14.refs_2_, ...), custom_call_target="tpu_custom_call" | custom-call | tf_op jit(solution)/shard_map/deliver/pallas_call | solution.py:497

commit v5 on v4

--- a/solution.py
+++ b/solution.py
@@ -12,6 +12,7 @@
 TOK = 2048
 SHARD = 128
 SPAN = 512
+RELAYED = (0, 1, 3)
 MESH = pl.DeviceIdType.MESH
 NEG = -1e30
 VMEM_LIMIT = 60 << 20
@@ -143,9 +144,11 @@
             pl.semaphore_wait(ready_sem.at[slot], 1)
 
     class Gather:
-        def __init__(self, shard):
+        def __init__(self, shard, half=None):
             self.shard = shard
+            self.half = half
             self.first = slots(16)
+            self.second = slots(4)
 
         def start(self):
             for dz in (1, 3, 2):
@@ -153,8 +156,18 @@
             self.along_y(0)
 
         def along_y(self, dz):
-            for dy in (1, 3, 2):
+            for dy in (1, 3) if self.half and dz in RELAYED else (1, 3, 2):
                 send(self.shard(dz, 0), self.shard(dz, 0), self.first + dz * 4 + dy, at(dy=dy))
+
+        def relay(self, dz):
+            for side, dy, slot in ((0, 1, self.first + dz * 4 + 2), (1, 3, self.second + dz)):
+                self.wait(dz, dy)
+                part = self.half(side, dz, dy)
+                send(part, part, slot, at(dy=dy))
+
+        def wait_halves(self, dz):
+            arrive(self.half(0, dz, 2), self.first + dz * 4 + 2)
+            arrive(self.half(1, dz, 2), self.second + dz)
 
         def wait(self, dz, dy):
             arrive(self.shard(dz, dy), self.first + dz * 4 + dy)
@@ -284,6 +297,7 @@
     for block in waiting:
         block_scores(*block)
 
+    act_z_later("far")
     scale = HD ** -0.5
     power = scale * 1.4426950408889634
     row_max = jnp.max(top[...], axis=1, keepdims=True)
@@ -338,7 +352,6 @@
     terms(0, 0)
     to_y(0, 1)
     to_y(0, 3)
-    act_z_later("far")
 
     inverse = 1.0 / jnp.sum(total, axis=1, keepdims=True)
     query_grad = dot(dsc[...], kv_all[0]) * (inverse * scale)
@@ -352,7 +365,10 @@
         index = ((z - dz) % 4) * 4 + (y - dy) % 4
         return pl.ds(pl.multiple_of(index * SHARD, SHARD), SHARD)
 
-    q_gather = Gather(lambda dz, dy: q_all.at[:, lanes_of(dz, dy)])
+    q_gather = Gather(
+        lambda dz, dy: q_all.at[:, lanes_of(dz, dy)],
+        lambda part, dz, dy: q_all.at[pl.ds(part * HD, HD), lanes_of(dz, dy)],
+    )
     q_gather.start()
 
     for dzh in (1, 3):
@@ -373,8 +389,12 @@
         other = jnp.where(side == part, 0, 1)
         for dz in (1, 3, 2):
             slot = dz * 2 + other
-            device = (((z + dz) % 4) * 4 + y, zh * 8 + (x - side + part) * 2 + core)
-            send(zx_send.at[part, (z + dz) % 4], zx_recv.at[slot], zx_slot + slot, device)
+            target = (z + dz) % 4
+            device = (target * 4 + y, zh * 8 + (x - side + part) * 2 + core)
+
+            @pl.when(target < z)
+            def _(target=target, slot=slot, device=device):
+                copy(zx_send.at[part, target], zx_recv.at[slot], zx_slot + slot, device).start()
 
         @pl.when(side != part)
         def _():
@@ -383,40 +403,53 @@
     for dz in (1, 2, 3):
         await_answer(("f", dz))
     to_zx(1)
+    for dz in (1, 3):
+        q_gather.wait(dz, 0)
+        q_gather.along_y(dz)
     to_zx(0)
     sends.append(copy(zx_send.at[0, 0], zx_recv.at[1], zx_slot + 1, flip(0)))
 
-    for dz in (1, 3, 2):
-        q_gather.wait(dz, 0)
-        q_gather.along_y(dz)
+    q_gather.wait(2, 0)
+    q_gather.along_y(2)
     arrive(act_shard(2, 0), act_first + 8)
     act_along_x(2)
 
-    kv_sum = own[side, 0, z]
-    for slot in range(1, 8):
-        arrive(zx_recv.at[slot], zx_slot + slot)
-    for slot in range(1, 8):
-        kv_sum = kv_sum + zx_recv[slot].astype(F32)
+    arrive(zx_recv.at[1], zx_slot + 1)
+    own[0, 1, 0] = own[side, 0, z] + zx_recv[1].astype(F32)
+    for dz in (1, 3, 2):
+        @pl.when((z - dz) % 4 > z)
+        def _(dz=dz):
+            for slot in (dz * 2, dz * 2 + 1):
+                arrive(zx_recv.at[slot], zx_slot + slot)
+                own[0, 1, 0] = own[0, 1, 0] + zx_recv[slot].astype(F32)
+
+    kv_sum = own[0, 1, 0]
     g_all[:, own_lanes] = kv_sum.astype(BF16)
     g_gather = Gather(lambda dz, dy: g_all.at[:, lanes_of(dz, dy)])
     g_gather.start()
     kv_out[...] = kv_sum.astype(BF16)
+    q_gather.relay(0)
+    q_gather.relay(1)
+    q_gather.relay(3)
+
+    for dz in (1, 3, 2):
+        g_gather.wait(dz, 0)
+        g_gather.along_y(dz)
 
     for dzh in (0, 1, 3):
         for dx in (1, 3, 2):
             arrive(act_shard(dzh, dx), act_first + dzh * 4 + dx)
             act_to_sibling(dzh, dx)
 
-    for dz in (1, 3, 2):
-        g_gather.wait(dz, 0)
-        g_gather.along_y(dz)
-
     for dx in (1, 3, 2):
         arrive(act_shard(2, dx), act_first + 8 + dx)
         act_to_sibling(2, dx)
     for dz in range(4):
-        for dy in (1, 3, 2):
-            q_gather.wait(dz, dy)
+        if dz in RELAYED:
+            q_gather.wait_halves(dz)
+        else:
+            for dy in (1, 3, 2):
+                q_gather.wait(dz, dy)
     for dzh in range(4):
         for dx in range(4):
             arrive(act_from_sibling(dzh, dx), act_sib + dzh * 4 + dx)
@@ -429,6 +462,11 @@
 
     for item in sends:
         item.wait_send()
+    for dz in (1, 2, 3):
+        @pl.when((z + dz) % 4 < z)
+        def _(dz=dz):
+            for slot in (dz * 2, dz * 2 + 1):
+                copy(zx_send.at[0, 0], zx_recv.at[slot], zx_slot + slot, at(dz=dz)).wait_send()
 
 
 def deliver(*refs):
@@ -482,8 +520,8 @@
             pltpu.VMEM((2, 3, 4, 64, HD), BF16),
             pltpu.VMEM((2, 4, 64, HD), BF16),
             pltpu.VMEM((8, 64, HD), BF16),
-            pltpu.SemaphoreType.DMA((128,)),
-            pltpu.SemaphoreType.DMA((128,)),
+            pltpu.SemaphoreType.DMA((152,)),
+            pltpu.SemaphoreType.DMA((152,)),
             pltpu.SemaphoreType.DMA((7,)),
             pltpu.SemaphoreType.REGULAR((12,)),
         ],

time: 50.7 us -> 50.5 us (level)
    pallas_call x1, Pallas kernels: 48.7 us -> 48.2 us  [per_device(): pl.pallas_call(body, name='attention_backward', out_shape=tuple((pltpu.VM...]
where the time goes in v5:
time: 50.5 us; the launch traced here: 49.6 us
  Pallas kernels  49 us (97%)
  between operations  0.64 us (1%)
    pallas_call x1, Pallas kernels, per_device(): pl.pallas_call(body, name='attention_backward', out_shape=tuple((pltpu.VM...  48.2 us

profile of v5, /device:TPU:6, one launch (start us, length us, event | category | flops | bytes accessed | tf_op | source)
XLA Modules:
  0.0 49.6 jit_solution(6534231069825702874)
XLA Ops:
  0.6 48.2 %attention_backward.1 = (bf16[128,256]{1,0:T(8,128)(2,1)S(1)}, bf16[64,128]{1,0:T(8,128)(2,1)S(1)}, bf16[512,256]{1,0:T(8,128)(2,1)S(1)}, bf16[64,512]{1,0:T(8,128)(2,1)S(1)}) custom-call(bf16[64,512]{1,0:T(8,128)(2,1)} %inputs.1, bf16[128,256]{1,0:T(8,128)(2,1)} %queries.1, bf16[128,1024]{1,0:T(8,128)(2,1)} %keys.1, bf16[128,1024]{1,0:T(8,128)(2,1)} %values.1, ...), custom_call_target="tpu_custom_call" | custom-call | flops 1400000000 | bytes 4194304 | tf_op jit(solution)/shard_map/attention_backward/pallas_call | solution.py:493
  48.8 0.8 %deliver.1 = (bf16[128,256]{1,0:T(8,128)(2,1)}, bf16[64,128]{1,0:T(8,128)(2,1)}, bf16[512,256]{1,0:T(8,128)(2,1)}, bf16[64,512]{1,0:T(8,128)(2,1)}) custom-call(bf16[128,256]{1,0:T(8,128)(2,1)S(1)} %get-tuple-element.12.refs_0_, bf16[64,128]{1,0:T(8,128)(2,1)S(1)} %get-tuple-element.13.refs_1_, bf16[512,256]{1,0:T(8,128)(2,1)S(1)} %get-tuple-element.14.refs_2_, ...), custom_call_target="tpu_custom_call" | custom-call | tf_op jit(solution)/shard_map/deliver/pallas_call | solution.py:535

commit v6 on v5

--- a/solution.py
+++ b/solution.py
@@ -444,16 +444,19 @@
     for dx in (1, 3, 2):
         arrive(act_shard(2, dx), act_first + 8 + dx)
         act_to_sibling(2, dx)
-    for dz in range(4):
+    for dzh in range(4):
+        for dx in range(4):
+            arrive(act_from_sibling(dzh, dx), act_sib + dzh * 4 + dx)
+    weight_q = jnp.zeros((256, 512), F32)
+    for dz in (0, 1, 3, 2):
         if dz in RELAYED:
             q_gather.wait_halves(dz)
         else:
             for dy in (1, 3, 2):
                 q_gather.wait(dz, dy)
-    for dzh in range(4):
-        for dx in range(4):
-            arrive(act_from_sibling(dzh, dx), act_sib + dzh * 4 + dx)
-    wq_out[...] = dot(q_all[...], act[...]).T.astype(BF16)
+        tokens = pl.ds(pl.multiple_of(((z - dz) % 4) * SPAN, SPAN), SPAN)
+        weight_q = weight_q + dot(q_all[:, tokens], act[tokens, :])
+    wq_out[...] = weight_q.T.astype(BF16)
 
     for dz in range(4):
         for dy in (1, 3, 2):

time: 50.5 us -> 50.5 us (level)
  no operation moved by 1% of the time
where the time goes in v6:
time: 50.5 us; the launch traced here: 49.6 us
  Pallas kernels  49 us (97%)
  between operations  0.64 us (1%)
    pallas_call x1, Pallas kernels, per_device(): pl.pallas_call(body, name='attention_backward', out_shape=tuple((pltpu.VM...  48.2 us

profile of v6, /device:TPU:6, one launch (start us, length us, event | category | flops | bytes accessed | tf_op | source)
XLA Modules:
  0.0 49.6 jit_solution(106993246921885705)
XLA Ops:
  0.6 48.2 %attention_backward.1 = (bf16[128,256]{1,0:T(8,128)(2,1)S(1)}, bf16[64,128]{1,0:T(8,128)(2,1)S(1)}, bf16[512,256]{1,0:T(8,128)(2,1)S(1)}, bf16[64,512]{1,0:T(8,128)(2,1)S(1)}) custom-call(bf16[64,512]{1,0:T(8,128)(2,1)} %inputs.1, bf16[128,256]{1,0:T(8,128)(2,1)} %queries.1, bf16[128,1024]{1,0:T(8,128)(2,1)} %keys.1, bf16[128,1024]{1,0:T(8,128)(2,1)} %values.1, ...), custom_call_target="tpu_custom_call" | custom-call | flops 1400000000 | bytes 4194304 | tf_op jit(solution)/shard_map/attention_backward/pallas_call | solution.py:496
  48.8 0.8 %deliver.1 = (bf16[128,256]{1,0:T(8,128)(2,1)}, bf16[64,128]{1,0:T(8,128)(2,1)}, bf16[512,256]{1,0:T(8,128)(2,1)}, bf16[64,512]{1,0:T(8,128)(2,1)}) custom-call(bf16[128,256]{1,0:T(8,128)(2,1)S(1)} %get-tuple-element.12.refs_0_, bf16[64,128]{1,0:T(8,128)(2,1)S(1)} %get-tuple-element.13.refs_1_, bf16[512,256]{1,0:T(8,128)(2,1)S(1)} %get-tuple-element.14.refs_2_, ...), custom_call_target="tpu_custom_call" | custom-call | tf_op jit(solution)/shard_map/deliver/pallas_call | solution.py:538
